TPU v7x, 512 devices: a whole 4x4x16 slice. The times are simulated.
512 devices in a mesh: dp: 64 (over z, y), tensor: 8 (over x, core).
Axes of the slice: x: 4, y: 4, z: 16, core: 2. Of those that a mesh axis runs over, the one named last changes fastest.
Arguments:
- patches: bfloat16 [16384, 1280], P('dp', 'tensor'), may hold values from -46 to 46
- send_counts: int32 [64, 64], replicated, may hold values from 0 to 4, as said below
- window_ids: int32 [128, 64], P('dp'), may hold values from 0 to 2, never falling along the last dimension, each value on 1 to 40 neighbouring positions
- token_shard: int32 [2048, 1], replicated, may hold values from 0 to 63; in each aligned block of 32 rows (0 to 31, 32 to 63, ...) at most 2 rows name the same one
- first_gain: float32 [1280], replicated, may hold values from 0.25 to 1.75
- qkv_weight: bfloat16 [1280, 3840], P(None, 'tensor'), may hold values from -1 to 1
- out_weight: bfloat16 [1280, 1280], P(None, 'tensor'), may hold values from -0.15625 to 0.15625
- merge_gain: float32 [1280], P('tensor'), may hold values from 0.25 to 1.75
- cotangent: bfloat16 [8192, 4, 1280], P('dp', None, 'tensor'), may hold values from -0.29882812 to 0.29882812
Outputs:
- merged_tokens: bfloat16 [8192, 4, 1280], P('dp', None, 'tensor')
- qkv_grad: bfloat16 [1280, 3840], P(None, 'tensor')
- out_grad: bfloat16 [1280, 1280], P(None, 'tensor')
- gain_grad: float32 [1280], P('tensor')
Inputs may be any that keep to these rules, and one draw needn't show every extreme that they name: `send_counts`: entry [i, j] is the number of live rows that source i sends to owner j; every column sums to exactly 128 and holds one entry equal to 4. `window_ids`: ids never fall along a row; each row is one tile of 64 rows of the owner layout. `token_shard`: among the 32 tokens of one owner (aligned blocks of 32 rows) no shard is named more than 2 times.
All inputs are finite; a program needn't handle non-finite values.
Results may differ from a plain program's by a relative error of at most 0.023.
Values may be sent and summed in bfloat16 or wider, within the bound.
A program may use at most 64 MiB of HBM per device.

v0:
```python
import math

import jax
import jax.numpy as jnp
from jax import lax
from jax.sharding import PartitionSpec as P

HD = 80
WIN = 64


EPS = 1e-06


def locate(counts, length):
    ends_at = jnp.cumsum(counts)
    starts = ends_at - counts
    position = jnp.arange(length, dtype=jnp.int32)
    source = jnp.sum((ends_at[None, :] <= position[:, None]).astype(jnp.int32), axis=1)
    source = jnp.minimum(source, counts.shape[0] - 1)
    offset = position - jnp.take(starts, source)
    filled = position < ends_at[-1]
    return (source, offset, filled)


def token_slots(token_shard, owners, tokens):
    target = token_shard[:, 0].reshape(owners, tokens)
    onehot = (target[:, :, None] == jnp.arange(owners, dtype=jnp.int32)[None, None, :]).astype(
        jnp.int32
    )
    earlier = jnp.cumsum(onehot, axis=1) - onehot
    order_in = jnp.sum(earlier * onehot, axis=2)
    counts = jnp.sum(onehot, axis=1)
    offsets = jnp.cumsum(counts, axis=0) - counts
    return (target, order_in, counts, offsets)


def attend(packed, windows, scaling):
    queries = packed[:, :, :, 0]
    key_rows = packed[:, :, :, 1]
    values = packed[:, :, :, 2]
    scores = (
        jnp.einsum("tqhe,tkhe->thqk", queries, key_rows, preferred_element_type=jnp.float32)
        * scaling
    )
    same_win = (windows[:, :, None] == windows[:, None, :])[:, None, :, :]
    scores = jnp.where(same_win, scores, -jnp.inf)
    highest = jnp.max(scores, axis=3, keepdims=True)
    raised = jnp.exp(scores - highest)
    weights = raised / jnp.sum(raised, axis=3, keepdims=True)
    rounded = weights.astype(jnp.bfloat16)
    output = jnp.einsum(
        "thqk,tkhe->tqhe", rounded, values, preferred_element_type=jnp.float32
    ).astype(jnp.bfloat16)
    return (output, weights, rounded)


def attend_back(grad_attn, packed, weights, rounded, scaling):
    queries = packed[:, :, :, 0]
    key_rows = packed[:, :, :, 1]
    values = packed[:, :, :, 2]
    dprobs = jnp.einsum("tqhe,tkhe->thqk", grad_attn, values, preferred_element_type=jnp.float32)
    dvalues = jnp.einsum(
        "thqk,tqhe->tkhe", rounded, grad_attn, preferred_element_type=jnp.float32
    ).astype(jnp.bfloat16)
    row_dot = jnp.sum(weights * dprobs, axis=3, keepdims=True)
    dscores = (weights * (dprobs - row_dot)).astype(jnp.bfloat16)
    dqueries = (
        jnp.einsum("thqk,tkhe->tqhe", dscores, key_rows, preferred_element_type=jnp.float32)
        * scaling
    ).astype(jnp.bfloat16)
    dkey_rows = (
        jnp.einsum("thqk,tqhe->tkhe", dscores, queries, preferred_element_type=jnp.float32)
        * scaling
    ).astype(jnp.bfloat16)
    return jnp.stack([dqueries, dkey_rows, dvalues], axis=3)


def ragged(buffers):
    return lax.all_to_all(buffers, "dp", split_axis=0, concat_axis=0, tiled=True)


def full_rows(shard_part):
    return lax.all_gather(shard_part, "tensor", axis=1, tiled=True)


def row_total(values):
    return lax.psum(values, "tensor")


def body(
    patches,
    send_counts,
    window_ids,
    token_shard,
    first_gain,
    qkv_weight,
    out_weight,
    merge_gain,
    cotangent,
):
    devices = lax.axis_size("dp")
    device = lax.axis_index("dp")
    rows_src, features = patches.shape
    rows_own = rows_src // 2
    slot_cap = rows_src // devices
    tokens = rows_own // 4
    lm_slots = cotangent.shape[0]
    token_cap = lm_slots // devices
    model_width = first_gain.shape[0]
    scaling = 1.0 / math.sqrt(HD)
    source_start = jnp.cumsum(send_counts, axis=1) - send_counts
    own_start = lax.dynamic_index_in_dim(source_start, device, 0, keepdims=False)
    pick_rows = jnp.minimum(
        own_start[:, None] + jnp.arange(slot_cap, dtype=jnp.int32)[None, :], rows_src - 1
    )
    outgoing = jnp.take(patches, pick_rows.reshape(-1), axis=0).reshape(devices, slot_cap, features)
    target, order_in, counts, offsets = token_slots(token_shard, devices, tokens)
    lm_counts = lax.dynamic_index_in_dim(counts, device, 1, keepdims=False)
    lm_offsets = lax.dynamic_index_in_dim(offsets, device, 1, keepdims=False)
    back_picks = jnp.minimum(
        lm_offsets[:, None] + jnp.arange(token_cap, dtype=jnp.int32)[None, :], lm_slots - 1
    )
    flat_cot = cotangent.reshape(lm_slots, 4 * features)
    returning = jnp.take(flat_cot, back_picks.reshape(-1), axis=0).reshape(
        devices, token_cap, 4 * features
    )
    arrived = ragged(outgoing)
    owner_counts = lax.dynamic_index_in_dim(send_counts, device, 1, keepdims=False)
    source, offset, filled_own = locate(owner_counts, rows_own)
    rows_in = jnp.take(
        arrived.reshape(devices * slot_cap, features), source * slot_cap + offset, axis=0
    )
    whole_rows = full_rows(rows_in)
    stream_all = whole_rows.astype(jnp.float32)
    inv_first = lax.rsqrt(jnp.mean(stream_all * stream_all, axis=1, keepdims=True) + EPS)
    normed_in = (stream_all * inv_first * first_gain).astype(jnp.bfloat16)
    packed = jnp.dot(normed_in, qkv_weight, preferred_element_type=jnp.float32).astype(jnp.bfloat16)
    heads_here = packed.shape[1] // (3 * HD)
    packed = packed.reshape(rows_own // WIN, WIN, heads_here, 3, HD)
    attn_tiles, weights, rounded = attend(packed, window_ids, scaling)
    attn_part = attn_tiles.reshape(rows_own, heads_here * HD)
    attn_all = full_rows(attn_part)
    residual = rows_in.astype(jnp.float32) + jnp.dot(
        attn_all, out_weight, preferred_element_type=jnp.float32
    )
    inv_second = lax.rsqrt(row_total(jnp.sum(residual * residual, axis=1)) / model_width + EPS)[
        :, None
    ]
    normed = (residual * inv_second * merge_gain).astype(jnp.bfloat16)
    own_target = lax.dynamic_index_in_dim(target, device, 0, keepdims=False)
    own_order = lax.dynamic_index_in_dim(order_in, device, 0, keepdims=False)
    slot_index = own_target * token_cap + own_order
    sending = (
        jnp.zeros((devices * token_cap, 4 * features), jnp.bfloat16)
        .at[slot_index]
        .set(normed.reshape(tokens, 4 * features))
    )
    landed = ragged(sending.reshape(devices, token_cap, 4 * features)).reshape(
        devices * token_cap, 4 * features
    )
    source_lm, offset_lm, filled_lm = locate(lm_counts, lm_slots)
    merged_rows = jnp.take(landed, source_lm * token_cap + offset_lm, axis=0)
    merged_tokens = jnp.where(filled_lm[:, None], merged_rows, jnp.zeros_like(merged_rows)).reshape(
        lm_slots, 4, features
    )
    came_back = ragged(returning).reshape(devices * token_cap, 4 * features)
    upstream_bf = jnp.take(came_back, slot_index, axis=0).reshape(rows_own, features)
    upstream = upstream_bf.astype(jnp.float32)
    gain_part = jnp.sum(upstream * residual * inv_second, axis=0)
    along_rows = row_total(jnp.sum(merge_gain * upstream * residual, axis=1))[:, None]
    dresidual = (
        merge_gain * upstream * inv_second - residual * along_rows * inv_second**3 / model_width
    ).astype(jnp.bfloat16)
    out_part = lax.dot_general(
        attn_all, dresidual, (((0,), (0,)), ((), ())), preferred_element_type=jnp.float32
    )
    spread = lax.dot_general(
        dresidual, out_weight, (((1,), (1,)), ((), ())), preferred_element_type=jnp.float32
    )
    attn_grad = lax.psum_scatter(
        spread.astype(jnp.bfloat16), "tensor", scatter_dimension=1, tiled=True
    )
    dpacked = attend_back(
        attn_grad.reshape(rows_own // WIN, WIN, heads_here, HD), packed, weights, rounded, scaling
    )
    dpacked = dpacked.reshape(rows_own, 3 * heads_here * HD)
    qkv_part = lax.dot_general(
        normed_in, dpacked, (((0,), (0,)), ((), ())), preferred_element_type=jnp.float32
    )
    qkv_total, out_sum, gain_grad = lax.psum((qkv_part, out_part, gain_part), "dp")
    qkv_grad = qkv_total.astype(jnp.bfloat16)
    return (merged_tokens, qkv_grad, out_sum.astype(jnp.bfloat16), gain_grad)


def solution(mesh):
    placed = (
        P("dp", "tensor"),
        P(),
        P("dp", None),
        P(),
        P(),
        P(None, "tensor"),
        P(None, "tensor"),
        P("tensor"),
        P("dp", None, "tensor"),
    )
    return jax.shard_map(
        body,
        mesh=mesh,
        in_specs=placed,
        out_specs=(P("dp", None, "tensor"), P(None, "tensor"), P(None, "tensor"), P("tensor")),
        check_vma=False,
    )
```

profile of v0, /device:TPU:6, one launch (start us, length us, event | category | flops | bytes accessed | tf_op | source)
XLA Modules:
  0.0 500.9 jit_solution(16632996736556446609)
XLA Ops:
  7.2 1.1 reduce_window_sum.43
  8.3 0.7 fusion.41
  9.2 1.0 copy.96
  10.2 1.2 gather_fusion
  11.6 0.8 broadcast_select_fusion.1
  12.4 18.7 %all-to-all-start = ((bf16[64,4,160]{2,1,0:T(4,128)(2,1)}), bf16[64,4,160]{2,1,0:T(4,128)(2,1)S(1)}, u32[]{:S(2)}, u32[]{:S(2)}) async-start(bf16[64,4,160]{2,1,0:T(4,128)(2,1)} %broadcast_select_fusion.1), calls=%async_computation | async-start | bytes 262144 | tf_op jit(solution)/shard_map/all_to_all | solution.py:80
  31.1 0.2 fusion.45
  31.3 0.5 broadcast.205
  31.8 0.7 reduce.12
  32.6 1.2 convert_reduce_fusion
  33.8 0.2 add_reduce_fusion
  34.1 0.2 fusion.37
  34.5 0.5 slice.34
  35.4 1.2 gather_fusion.3
  37.2 0.9 gather_fusion.6
  38.2 0.7 reshape.223
  39.1 1.2 gather_fusion.4
  40.4 0.5 compare_and_fusion.1
  41.0 7.8 %all-to-all-done = bf16[64,4,160]{2,1,0:T(4,128)(2,1)S(1)} async-done(((bf16[64,4,160]{2,1,0:T(4,128)(2,1)}), bf16[64,4,160]{2,1,0:T(4,128)(2,1)S(1)}, u32[]{:S(2)}, u32[]{:S(2)}) %all-to-all-start) | async-done | bytes 81952 | tf_op jit(solution)/shard_map/all_to_all | solution.py:80
  48.8 7.3 %all-to-all-start.2 = ((bf16[64,2,640]{2,1,0:T(2,128)(2,1)}), bf16[64,2,640]{2,1,0:T(2,128)(2,1)S(1)}, u32[]{:S(2)}, u32[]{:S(2)}) async-start(bf16[64,2,640]{2,1,0:T(2,128)(2,1)} %reshape.223), calls=%async_computation.2 | async-start | bytes 327680 | tf_op jit(solution)/shard_map/all_to_all | solution.py:80
  56.2 0.8 gather_fusion.1
  57.2 12.9 %all_gather.6 = bf16[128,1280]{0,1:T(8,128)(2,1)S(1)} all-gather(bf16[128,160]{0,1:T(8,128)(2,1)S(1)} %broadcast_select_fusion.3), channel_id=1, replica_groups=mesh['dp'=64,'tensor'=8] {'tensor'}, dimensions={1}, use_global_device_ids=true | all-gather | bytes 368640 | tf_op jit(solution)/shard_map/all_gather | solution.py:84
  70.1 0.2 fusion.14
  70.3 0.6 convolution_convert_fusion.1
  71.0 0.2 fusion.46
  71.6 0.2 fusion.47
  72.0 0.2 fusion.10
  72.4 12.9 %all_gather.7 = bf16[128,1280]{0,1:T(8,128)(2,1)S(1)} all-gather(bf16[128,160]{0,1:T(8,128)(2,1)S(1)} %reshape.217), channel_id=1, replica_groups=mesh['dp'=64,'tensor'=8] {'tensor'}, dimensions={1}, use_global_device_ids=true | all-gather | bytes 368640 | tf_op jit(solution)/shard_map/all_gather | solution.py:84
  85.3 0.3 multiply_reduce_fusion.1
  85.6 10.9 %psum.35 = f32[128]{0:T(128)S(1)} all-reduce(f32[128]{0:T(128)S(1)} %get-tuple-element.35), channel_id=1, replica_groups=mesh['dp'=64,'tensor'=8] {'tensor'}, use_global_device_ids=true, to_apply=%region_11.13 | all-reduce | flops 128 | bytes 1024 | tf_op jit(solution)/shard_map/psum | solution.py:88
  96.6 0.6 gather_fusion.2
  97.6 13.2 %psum.36 = f32[128]{0:T(128)S(1)} all-reduce(f32[128]{0:T(128)S(1)} %get-tuple-element.11), channel_id=1, replica_groups=mesh['dp'=64,'tensor'=8] {'tensor'}, use_global_device_ids=true, to_apply=%region_16.19 | all-reduce | flops 128 | bytes 1024 | tf_op jit(solution)/shard_map/psum | solution.py:88
  111.1 0.8 scatter_custom_fusion
  111.9 0.7 reshape.219
  112.7 15.1 %all-to-all-start.1 = ((bf16[64,2,640]{2,1,0:T(2,128)(2,1)}), bf16[64,2,640]{2,1,0:T(2,128)(2,1)S(1)}, u32[]{:S(2)}, u32[]{:S(2)}) async-start(bf16[64,2,640]{2,1,0:T(2,128)(2,1)} %reshape.219), calls=%async_computation.1 | async-start | bytes 327680 | tf_op jit(solution)/shard_map/all_to_all | solution.py:80
  127.8 0.2 reduce-scatter.2.cloned.1.call-start
  128.0 1.1 convolution_convert_fusion
  129.1 1.2 iota_compare_fusion.4
  130.3 0.3 fusion.48
  130.6 16.8 %all-to-all-done.1 = bf16[64,2,640]{2,1,0:T(2,128)(2,1)S(1)} async-done(((bf16[64,2,640]{2,1,0:T(2,128)(2,1)}), bf16[64,2,640]{2,1,0:T(2,128)(2,1)S(1)}, u32[]{:S(2)}, u32[]{:S(2)}) %all-to-all-start.1) | async-done | bytes 163872 | tf_op jit(solution)/shard_map/all_to_all | solution.py:80
  147.5 0.9 gather_fusion.5
  148.5 0.8 copy.104
  149.3 19.7 %reduce-scatter.2.cloned.1.call-done = bf16[128,160]{0,1:T(8,128)(2,1)} async-done(((bf16[128,1280]{0,1:T(8,128)(2,1)}), bf16[128,160]{0,1:T(8,128)(2,1)}) %reduce-scatter.2.cloned.1.call-update) | async-done | bytes 40976 | tf_op jit(solution)/shard_map/reduce_scatter | solution.py:181
  169.0 0.9 reshape.225
  170.0 0.2 multiply_reduce_fusion
  170.2 0.2 fusion.13
  171.2 2.0 fusion.20
  173.2 320.8 %all-reduce.2 = (bf16[1280,480]{0,1:T(8,128)(2,1)}, bf16[1280,160]{0,1:T(8,128)(2,1)}, f32[160]{0:T(256)}) all-reduce(f32[1280,480]{0,1:T(8,128)} %fusion.20, f32[1280,160]{0,1:T(8,128)S(1)} %fusion.48, f32[160]{0:T(256)S(1)} %get-tuple-element.10), channel_id=1, replica_groups=mesh['dp'=64,'tensor'=8] {'dp'}, use_global_device_ids=true, to_apply=%region_19.22 | all-reduce | flops 819360 | bytes 4916480 | tf_op jit(solution)/shard_map/psum | solution.py:191
  (92 shorter events, 4.9 us)
Async XLA Ops:
  7.2 63.1 %copy-start = (bf16[1280,480]{0,1:T(8,128)(2,1)S(1)}, bf16[1280,480]{0,1:T(8,128)(2,1)}, u32[]{:S(2)}) copy-start(bf16[1280,480]{0,1:T(8,128)(2,1)} %param.18) | copy-start | bytes 3686404
  7.2 23.9 %copy-start.3 = (s32[64,64]{1,0:T(8,128)S(1)}, s32[64,64]{1,0:T(8,128)}, u32[]{:S(2)}) copy-start(s32[64,64]{1,0:T(8,128)} %param.14) | copy-start | bytes 49156
  7.2 24.6 %copy-start.5 = (s32[2048,1]{0,1:T(1,128)S(1)}, s32[2048,1]{0,1:T(1,128)}, u32[]{:S(2)}) copy-start(s32[2048,1]{0,1:T(1,128)} %param.16) | copy-start | bytes 24580
  11.4 25.6 %copy-start.2 = (bf16[128,4,160]{0,2,1:T(8,128)(2,1)S(1)}, bf16[128,4,160]{0,2,1:T(8,128)(2,1)}, u32[]{:S(2)}) copy-start(bf16[128,4,160]{0,2,1:T(8,128)(2,1)} %param.21) | copy-start | bytes 491524
  12.4 36.4 %all-to-all-start = ((bf16[64,4,160]{2,1,0:T(4,128)(2,1)}), bf16[64,4,160]{2,1,0:T(4,128)(2,1)S(1)}, u32[]{:S(2)}, u32[]{:S(2)}) async-start(bf16[64,4,160]{2,1,0:T(4,128)(2,1)} %broadcast_select_fusion.1), calls=%async_computation | async-start | bytes 262144 | tf_op jit(solution)/shard_map/all_to_all | solution.py:80
  37.2 3.7 copy-start.7
  39.1 31.2 %copy-start.4 = (f32[1280]{0:T(1024)S(1)}, f32[1280]{0:T(1024)}, u32[]{:S(2)}) copy-start(f32[1280]{0:T(1024)} %param.17) | copy-start | bytes 15364
  48.8 47.7 %all-to-all-start.2 = ((bf16[64,2,640]{2,1,0:T(2,128)(2,1)}), bf16[64,2,640]{2,1,0:T(2,128)(2,1)S(1)}, u32[]{:S(2)}, u32[]{:S(2)}) async-start(bf16[64,2,640]{2,1,0:T(2,128)(2,1)} %reshape.223), calls=%async_computation.2 | async-start | bytes 327680 | tf_op jit(solution)/shard_map/all_to_all | solution.py:80
  70.3 0.9 copy-start.9
  71.2 14.1 %copy-start.1 = (bf16[1280,160]{0,1:T(8,128)(2,1)S(1)}, bf16[1280,160]{0,1:T(8,128)(2,1)}, u32[]{:S(2)}) copy-start(bf16[1280,160]{0,1:T(8,128)(2,1)} %param.19) | copy-start | bytes 1228804
  72.2 25.3 %copy-start.6 = (f32[160]{0:T(256)S(1)}, f32[160]{0:T(256)}, u32[]{:S(2)}) copy-start(f32[160]{0:T(256)} %param.20) | copy-start | bytes 1924
  97.5 32.8 %copy-start.8 = (s32[128]{0:T(128)S(1)}, s32[128]{0:T(128)}, u32[]{:S(2)}) copy-start(s32[128]{0:T(128)} %get-tuple-element.20) | copy-start | bytes 1540
  112.7 34.7 %all-to-all-start.1 = ((bf16[64,2,640]{2,1,0:T(2,128)(2,1)}), bf16[64,2,640]{2,1,0:T(2,128)(2,1)S(1)}, u32[]{:S(2)}, u32[]{:S(2)}) async-start(bf16[64,2,640]{2,1,0:T(2,128)(2,1)} %reshape.219), calls=%async_computation.1 | async-start | bytes 327680 | tf_op jit(solution)/shard_map/all_to_all | solution.py:80
  127.8 41.3 %reduce-scatter.2.cloned.1.call-start = ((), (), s32[]{:S(2)}) async-start(), calls=%async_computation.4 | async-start | bytes 368640 | tf_op jit(solution)/shard_map/reduce_scatter | solution.py:181
  130.6 17.8 %copy-start.11 = (pred[128]{0:T(512)(128)(4,1)S(1)}, pred[128]{0:T(512)(128)(4,1)}, u32[]{:S(2)}) copy-start(pred[128]{0:T(512)(128)(4,1)} %iota_compare_fusion.4) | copy-start | bytes 388
  170.2 1.0 copy-start.10
Sparse Core Ops, SparseCore 0:
  132.0 37.0 reduce-scatter.1
where the time goes:
time: 501 us
  blocking collectives  371 us (74%)
  waiting for transfers between devices  44.3 us (9%)
  starting transfers between devices  41.4 us (8%)
  local copies, waits for them, and re-layouts  16.1 us (3%)
  between operations  14.6 us (3%)
  other arithmetic  8.45 us (2%)
  matrix products  5.38 us (1%)
    psum x1, blocking collectives, body(): lax.psum((qkv_part, out_part, gain_part), 'dp')  321 us
    all_to_all x3, starting transfers between devices, ragged(): lax.all_to_all(buffers, 'dp', split_axis=0, concat_axis=0, tiled=True)  41.1 us
    all_gather x2, blocking collectives, full_rows(): return lax.all_gather(shard_part, 'tensor', axis=1, tiled=True)  25.8 us
    all_to_all x3, waiting for transfers between devices, ragged(): lax.all_to_all(buffers, 'dp', split_axis=0, concat_axis=0, tiled=True)  24.6 us
    psum x2, blocking collectives, row_total(): return lax.psum(values, 'tensor')  24.1 us
    reduce_scatter x1, waiting for transfers between devices, body(): lax.psum_scatter(spread.astype(jnp.bfloat16), 'tensor', scatter_dimension...  19.7 us
  transfers between devices with their start and end apart: 4, of which 3 were waited for; matrix products, arithmetic and copies ran while one was open for 4% of the time, Pallas kernels for 0%

commit v1 on v0

--- a/solution.py
+++ b/solution.py
@@ -1,8 +1,11 @@
+import functools
 import math
 
 import jax
 import jax.numpy as jnp
 from jax import lax
+from jax.experimental import pallas as pl
+from jax.experimental.pallas import tpu as pltpu
 from jax.sharding import PartitionSpec as P
 
 HD = 80
@@ -86,6 +89,383 @@
 
 def row_total(values):
     return lax.psum(values, "tensor")
+
+
+MESH = pl.DeviceIdType.MESH
+
+
+def reduce_kernel(
+    nz,
+    ny,
+    lhs_ref,
+    rhs_ref,
+    gain_ref,
+    qkv_ref,
+    out_ref,
+    gsum_ref,
+    part,
+    full,
+    c_buf,
+    n_buf,
+    p_buf,
+    zs_up,
+    zs_dn,
+    zr_up,
+    zr_dn,
+    y_ss,
+    y_rs,
+    z_ss,
+    z_rs,
+    g_ss,
+    g_rs,
+    f_ss,
+    f_rs,
+):
+    half = nz // 2
+    width, cols = lhs_ref.shape[1], rhs_ref.shape[1]
+    per_row = cols // 128
+    live = (width // 16) * per_row
+    tiles = part.shape[0]
+    per = tiles // (nz * ny)
+    me = lax.axis_index("dp")
+    z, y = me // ny, lax.rem(me, ny)
+
+    def dev(zz, yy):
+        return {"dp": lax.rem(zz + nz, nz) * ny + lax.rem(yy + ny, ny)}
+
+    up_y, dn_y, up_z, dn_z = dev(z, y + 1), dev(z, y - 1), dev(z + 1, y), dev(z - 1, y)
+    barrier = pltpu.get_barrier_semaphore()
+    for peer in (up_y, dn_y, up_z, dn_z):
+        pl.semaphore_signal(barrier, inc=1, device_id=peer, device_id_type=MESH)
+
+    block = 128
+    per_block = (block // 16) * per_row
+
+    def products(b, carry):
+        got = lax.dot_general(
+            lhs_ref[:, pl.ds(pl.multiple_of(b * block, block), block)],
+            rhs_ref[...],
+            (((0,), (0,)), ((), ())),
+            preferred_element_type=jnp.float32,
+        ).astype(jnp.bfloat16)
+        for i in range(block // 16):
+            for c in range(per_row):
+                part[b * per_block + i * per_row + c] = got[16 * i : 16 * i + 16, 128 * c : 128 * c + 128]
+        return carry
+
+    lax.fori_loop(0, width // block, products, 0)
+    part[pl.ds(live, tiles - live)] = jnp.zeros((tiles - live, 16, 128), jnp.bfloat16)
+    part[live] = gain_ref[...].astype(jnp.bfloat16)
+
+    pl.semaphore_wait(barrier, 4)
+
+    def spot(yy, d):
+        return pl.ds((lax.rem(yy + ny, ny) * nz + d) * per, per)
+
+    def copy(src, dst, ss, rs, peer):
+        return pltpu.make_async_remote_copy(
+            src_ref=src, dst_ref=dst, send_sem=ss, recv_sem=rs, device_id=peer, device_id_type=MESH
+        )
+
+    def c_copy(d, fwd):
+        src = part.at[spot(y + 2, d)]
+        return copy(src, c_buf.at[d], y_ss.at[0, d], y_rs.at[0, d], up_y if fwd else dn_y)
+
+    def n_copy(d, fwd):
+        src = part.at[spot(y - 1 if fwd else y + 1, d)]
+        return copy(src, n_buf.at[d], y_ss.at[1, d], y_rs.at[1, d], dn_y if fwd else up_y)
+
+    def p_copy(d, fwd):
+        src = part.at[spot(y + 1 if fwd else y - 1, d)]
+        return copy(src, p_buf.at[d], y_ss.at[2, d], y_rs.at[2, d], up_y if fwd else dn_y)
+
+    def both(d, act):
+        even = lax.rem(d, 2) == 0
+
+        @pl.when(even)
+        def _():
+            act(True)
+
+        @pl.when(jnp.logical_not(even))
+        def _():
+            act(False)
+
+    def y_first(d):
+        def act(fwd):
+            c_copy(d, fwd).start()
+            n_copy(d, fwd).start()
+
+        both(d, act)
+
+    def y_second(d):
+        def act(fwd):
+            c_copy(d, fwd).wait_recv()
+            here = spot(y + 1 if fwd else y - 1, d)
+            total = part[here].astype(jnp.float32) + c_buf[d].astype(jnp.float32)
+            part[here] = total.astype(jnp.bfloat16)
+            p_copy(d, fwd).start()
+
+        both(d, act)
+
+    def y_sum(d):
+        n_copy(d, True).wait_recv()
+        p_copy(d, True).wait_recv()
+        return (
+            part[spot(y, d)].astype(jnp.float32)
+            + n_buf[d].astype(jnp.float32)
+            + p_buf[d].astype(jnp.float32)
+        )
+
+    def up_dest(k):
+        return lax.rem(z + half - k, nz)
+
+    def dn_dest(k):
+        return lax.rem(z + nz - half + k, nz)
+
+    def group(k, act):
+        act(up_dest(k))
+
+        @pl.when(jnp.logical_and(k > 0, k < half))
+        def _():
+            act(dn_dest(k))
+
+    def zu_copy(k):
+        return copy(zs_up.at[k], zr_up.at[k], z_ss.at[0, k], z_rs.at[0, k], up_z)
+
+    def zd_copy(k):
+        return copy(zs_dn.at[k], zr_dn.at[k], z_ss.at[1, k], z_rs.at[1, k], dn_z)
+
+    ahead_first, ahead_second = 3, 1
+
+    def first_group(k, carry):
+        group(k, y_first)
+        return carry
+
+    def second_group(k, carry):
+        group(k, y_second)
+        return carry
+
+    lax.fori_loop(0, ahead_first, first_group, 0)
+    lax.fori_loop(0, ahead_second, second_group, 0)
+
+    def z_step(k, carry):
+        @pl.when(k + ahead_first <= half)
+        def _():
+            group(k + ahead_first, y_first)
+
+        @pl.when(k + ahead_second <= half)
+        def _():
+            group(k + ahead_second, y_second)
+
+        @pl.when(k == 0)
+        def _():
+            zs_up[k] = y_sum(up_dest(k)).astype(jnp.bfloat16)
+            zu_copy(k).start()
+
+        @pl.when(k > 0)
+        def _():
+            total = y_sum(up_dest(k))
+            zu_copy(k - 1).wait_recv()
+            zs_up[k] = (total + zr_up[k - 1].astype(jnp.float32)).astype(jnp.bfloat16)
+            zu_copy(k).start()
+            total = y_sum(dn_dest(k))
+
+            @pl.when(k > 1)
+            def _():
+                zd_copy(k - 1).wait_recv()
+                zs_dn[k] = (total + zr_dn[k - 1].astype(jnp.float32)).astype(jnp.bfloat16)
+
+            @pl.when(k == 1)
+            def _():
+                zs_dn[k] = total.astype(jnp.bfloat16)
+
+            zd_copy(k).start()
+
+        return carry
+
+    lax.fori_loop(0, half, z_step, 0)
+    total = y_sum(z)
+    zu_copy(half - 1).wait_recv()
+    zd_copy(half - 1).wait_recv()
+    own = spot(y, z)
+    full[own] = (
+        total + zr_up[half - 1].astype(jnp.float32) + zr_dn[half - 1].astype(jnp.float32)
+    ).astype(jnp.bfloat16)
+
+    def gz_up(s):
+        at = full.at[spot(y, lax.rem(z - s + nz, nz))]
+        return copy(at, at, g_ss.at[0, s], g_rs.at[0, s], up_z)
+
+    def gz_dn(s):
+        at = full.at[spot(y, lax.rem(z + s, nz))]
+        return copy(at, at, g_ss.at[1, s], g_rs.at[1, s], dn_z)
+
+    def gz_up_in(s):
+        at = full.at[spot(y, lax.rem(z - s - 1 + nz, nz))]
+        return copy(at, at, g_ss.at[0, s], g_rs.at[0, s], up_z)
+
+    def gz_dn_in(s):
+        at = full.at[spot(y, lax.rem(z + s + 1, nz))]
+        return copy(at, at, g_ss.at[1, s], g_rs.at[1, s], dn_z)
+
+    def ya_copy(d, yy):
+        at = full.at[spot(yy, d)]
+        return copy(at, at, f_ss.at[0, d], f_rs.at[0, d], up_y)
+
+    def yb_copy(d, yy):
+        at = full.at[spot(yy, d)]
+        return copy(at, at, f_ss.at[1, d], f_rs.at[1, d], dn_y)
+
+    def yf_copy(d, fwd):
+        at = full.at[spot(y - 1 if fwd else y + 1, d)]
+        return copy(at, at, f_ss.at[2, d], f_rs.at[2, d], up_y if fwd else dn_y)
+
+    def spread(d):
+        ya_copy(d, y).start()
+        yb_copy(d, y).start()
+
+    def onward(d):
+        def act(fwd):
+            if fwd:
+                ya_copy(d, y - 1).wait_recv()
+            else:
+                yb_copy(d, y + 1).wait_recv()
+            yf_copy(d, fwd).start()
+
+        both(d, act)
+
+    def g_step(s, carry):
+        @pl.when(s > 0)
+        def _():
+            gz_up_in(s - 1).wait_recv()
+
+        gz_up(s).start()
+
+        @pl.when(jnp.logical_and(s > 0, s < half))
+        def _():
+            gz_dn_in(s - 1).wait_recv()
+
+        @pl.when(s < half - 1)
+        def _():
+            gz_dn(s).start()
+
+        spread(lax.rem(z - s + nz, nz))
+
+        @pl.when(s > 0)
+        def _():
+            spread(lax.rem(z + s, nz))
+
+        @pl.when(s > 1)
+        def _():
+            onward(lax.rem(z - s + 1 + nz, nz))
+            onward(lax.rem(z + s - 1, nz))
+
+        @pl.when(s == 1)
+        def _():
+            onward(z)
+
+        return carry
+
+    lax.fori_loop(0, half, g_step, 0)
+    gz_up_in(half - 1).wait_recv()
+    spread(lax.rem(z + half, nz))
+    onward(lax.rem(z - half + 1 + nz, nz))
+    onward(lax.rem(z + half - 1, nz))
+    onward(lax.rem(z + half, nz))
+
+    def arrivals(d, carry):
+        def act(fwd):
+            if fwd:
+                yb_copy(d, y + 1).wait_recv()
+            else:
+                ya_copy(d, y - 1).wait_recv()
+            at = full.at[spot(y + 2, d)]
+            copy(at, at, f_ss.at[2, d], f_rs.at[2, d], up_y).wait_recv()
+
+        both(d, act)
+        return carry
+
+    lax.fori_loop(0, nz, arrivals, 0)
+
+    def unpack(r, carry):
+        rows = pl.ds(pl.multiple_of(r * 16, 16), 16)
+        for c in range(3):
+            qkv_ref[rows, 128 * c : 128 * c + 128] = full[r * per_row + c]
+        mixed = full[r * per_row + 3]
+        qkv_ref[rows, 384:480] = mixed[:, :96]
+        out_ref[rows, 128:160] = mixed[:, 96:]
+        out_ref[rows, 0:128] = full[r * per_row + 4]
+        return carry
+
+    lax.fori_loop(0, width // 16, unpack, 0)
+    gsum_ref[...] = full[live].astype(jnp.float32)
+
+    def drain_y(d, carry):
+        for j in range(3):
+            copy(c_buf.at[d], c_buf.at[d], y_ss.at[j, d], y_rs.at[j, d], up_y).wait_send()
+            copy(c_buf.at[d], c_buf.at[d], f_ss.at[j, d], f_rs.at[j, d], up_y).wait_send()
+        return carry
+
+    lax.fori_loop(0, nz, drain_y, 0)
+
+    def drain_z(k, carry):
+        zu_copy(k).wait_send()
+        gz_up(k).wait_send()
+
+        @pl.when(k > 0)
+        def _():
+            zd_copy(k).wait_send()
+
+        @pl.when(k < half - 1)
+        def _():
+            gz_dn(k).wait_send()
+
+        return carry
+
+    lax.fori_loop(0, half, drain_z, 0)
+
+
+def reduce_gradients(nz, ny, lhs, rhs, gain):
+    width, cols = lhs.shape[1], rhs.shape[1]
+    live = (width // 16) * (cols // 128)
+    per = -(-(live + 1) // (nz * ny))
+    half = nz // 2
+    bf16 = jnp.bfloat16
+    vmem = pl.BlockSpec(memory_space=pltpu.VMEM)
+    sems = pltpu.SemaphoreType.DMA
+    return pl.pallas_call(
+        functools.partial(reduce_kernel, nz, ny),
+        out_shape=(
+            jax.ShapeDtypeStruct((width, 480), bf16),
+            jax.ShapeDtypeStruct((width, 160), bf16),
+            jax.ShapeDtypeStruct((16, 128), jnp.float32),
+        ),
+        in_specs=[vmem] * 3,
+        out_specs=(vmem,) * 3,
+        scratch_shapes=[
+            pltpu.VMEM((per * nz * ny, 16, 128), bf16),
+            pltpu.VMEM((per * nz * ny, 16, 128), bf16),
+            pltpu.VMEM((nz, per, 16, 128), bf16),
+            pltpu.VMEM((nz, per, 16, 128), bf16),
+            pltpu.VMEM((nz, per, 16, 128), bf16),
+            pltpu.VMEM((half, per, 16, 128), bf16),
+            pltpu.VMEM((half, per, 16, 128), bf16),
+            pltpu.VMEM((half, per, 16, 128), bf16),
+            pltpu.VMEM((half, per, 16, 128), bf16),
+            sems((3, nz)),
+            sems((3, nz)),
+            sems((2, half)),
+            sems((2, half)),
+            sems((2, half)),
+            sems((2, half)),
+            sems((3, nz)),
+            sems((3, nz)),
+        ],
+        compiler_params=pltpu.CompilerParams(
+            collective_id=0, has_side_effects=True, vmem_limit_bytes=48 * 1024 * 1024
+        ),
+        name="reduce_gradients",
+    )(lhs, rhs, gain)
 
 
 def body(
@@ -172,9 +552,6 @@
     dresidual = (
         merge_gain * upstream * inv_second - residual * along_rows * inv_second**3 / model_width
     ).astype(jnp.bfloat16)
-    out_part = lax.dot_general(
-        attn_all, dresidual, (((0,), (0,)), ((), ())), preferred_element_type=jnp.float32
-    )
     spread = lax.dot_general(
         dresidual, out_weight, (((1,), (1,)), ((), ())), preferred_element_type=jnp.float32
     )
@@ -185,12 +562,19 @@
         attn_grad.reshape(rows_own // WIN, WIN, heads_here, HD), packed, weights, rounded, scaling
     )
     dpacked = dpacked.reshape(rows_own, 3 * heads_here * HD)
-    qkv_part = lax.dot_general(
-        normed_in, dpacked, (((0,), (0,)), ((), ())), preferred_element_type=jnp.float32
-    )
-    qkv_total, out_sum, gain_grad = lax.psum((qkv_part, out_part, gain_part), "dp")
-    qkv_grad = qkv_total.astype(jnp.bfloat16)
-    return (merged_tokens, qkv_grad, out_sum.astype(jnp.bfloat16), gain_grad)
+    lhs = jnp.concatenate([normed_in, attn_all], axis=0)
+    swapped = jnp.concatenate([dresidual[:, 128:], dresidual[:, :128]], axis=1)
+    rhs = jnp.concatenate(
+        [
+            jnp.pad(dpacked, ((0, 0), (0, features))),
+            jnp.pad(swapped, ((0, 0), (dpacked.shape[1], 0))),
+        ],
+        axis=0,
+    )
+    gain_tile = jnp.pad(gain_part, (0, 16 * 128 - features)).reshape(16, 128)
+    qkv_grad, out_grad, gain_sum = reduce_gradients(devices // 4, 4, lhs, rhs, gain_tile)
+    gain_grad = gain_sum.reshape(-1)[:features]
+    return (merged_tokens, qkv_grad, out_grad, gain_grad)
 
 
 def solution(mesh):

time: 501 us -> 265 us (0.53)
  blocking collectives: 371 us -> 49.9 us
  Pallas kernels: 0 us -> 78.5 us
    psum x1 -> x0, blocking collectives: 321 us -> none  [body(): lax.psum((qkv_part, out_part, gain_part), 'dp')]
    pallas_call x0 -> x1, Pallas kernels: none -> 78.5 us  [reduce_gradients(): pl.pallas_call(functools.partial(reduce_kernel, nz, ny), out_shape=(jax.S...]
  transfers between devices with their start and end apart: 4 -> 4, of which waited for: 3 -> 3; matrix products, arithmetic and copies ran while one was open for 4% -> 7% of each run, Pallas kernels for 0% -> 0%
where the time goes in v1:
time: 265 us; the launch traced here: 261 us
  Pallas kernels  78.5 us (30%)
  blocking collectives  49.9 us (19%)
  waiting for transfers between devices  45.5 us (17%)
  starting transfers between devices  41.5 us (16%)
  local copies, waits for them, and re-layouts  20.1 us (8%)
  between operations  14.6 us (6%)
  other arithmetic  8.32 us (3%)
  matrix products  3.08 us (1%)
    pallas_call x1, Pallas kernels, reduce_gradients(): pl.pallas_call(functools.partial(reduce_kernel, nz, ny), out_shape=(jax.S...  78.5 us
    all_to_all x3, starting transfers between devices, ragged(): lax.all_to_all(buffers, 'dp', split_axis=0, concat_axis=0, tiled=True)  41.3 us
    all_gather x2, blocking collectives, full_rows(): return lax.all_gather(shard_part, 'tensor', axis=1, tiled=True)  25.8 us
    all_to_all x3, waiting for transfers between devices, ragged(): lax.all_to_all(buffers, 'dp', split_axis=0, concat_axis=0, tiled=True)  25.7 us
    psum x2, blocking collectives, row_total(): return lax.psum(values, 'tensor')  24.1 us
    reduce_scatter x1, waiting for transfers between devices, body(): lax.psum_scatter(spread.astype(jnp.bfloat16), 'tensor', scatter_dimension...  19.7 us
  transfers between devices with their start and end apart: 4, of which 3 were waited for; matrix products, arithmetic and copies ran while one was open for 7% of the time, Pallas kernels for 0%

profile of v1, /device:TPU:6, one launch (start us, length us, event | category | flops | bytes accessed | tf_op | source)
XLA Modules:
  0.0 261.4 jit_solution(11094411172414783163)
XLA Ops:
  7.2 1.1 reduce_window_sum.43
  8.3 0.7 fusion.43
  9.2 1.0 copy.114
  10.2 1.2 gather_fusion
  11.6 0.8 broadcast_select_fusion.1
  12.4 18.7 %all-to-all-start = ((bf16[64,4,160]{2,1,0:T(4,128)(2,1)}), bf16[64,4,160]{2,1,0:T(4,128)(2,1)S(1)}, u32[]{:S(2)}, u32[]{:S(2)}) async-start(bf16[64,4,160]{2,1,0:T(4,128)(2,1)} %broadcast_select_fusion.1), calls=%async_computation | async-start | bytes 262144 | tf_op jit(solution)/shard_map/all_to_all | solution.py:83
  31.3 0.5 broadcast.221
  31.8 0.7 reduce.12
  32.6 1.2 convert_reduce_fusion
  33.8 0.2 add_reduce_fusion
  34.1 0.2 fusion.39
  34.5 0.5 slice.46
  35.4 1.2 gather_fusion.3
  37.2 0.9 gather_fusion.6
  38.2 0.7 reshape.229
  39.1 1.2 gather_fusion.4
  40.4 0.7 iota_compare_fusion.6
  41.2 7.6 %all-to-all-done = bf16[64,4,160]{2,1,0:T(4,128)(2,1)S(1)} async-done(((bf16[64,4,160]{2,1,0:T(4,128)(2,1)}), bf16[64,4,160]{2,1,0:T(4,128)(2,1)S(1)}, u32[]{:S(2)}, u32[]{:S(2)}) %all-to-all-start) | async-done | bytes 81952 | tf_op jit(solution)/shard_map/all_to_all | solution.py:83
  48.8 7.5 %all-to-all-start.2 = ((bf16[64,2,640]{2,1,0:T(2,128)(2,1)}), bf16[64,2,640]{2,1,0:T(2,128)(2,1)S(1)}, u32[]{:S(2)}, u32[]{:S(2)}) async-start(bf16[64,2,640]{2,1,0:T(2,128)(2,1)} %reshape.229), calls=%async_computation.2 | async-start | bytes 327680 | tf_op jit(solution)/shard_map/all_to_all | solution.py:83
  56.4 0.8 gather_fusion.1
  57.4 12.9 %all_gather.6 = bf16[128,1280]{0,1:T(8,128)(2,1)S(1)} all-gather(bf16[128,160]{0,1:T(8,128)(2,1)S(1)} %copy.115), channel_id=1, replica_groups=mesh['dp'=64,'tensor'=8] {'tensor'}, dimensions={1}, use_global_device_ids=true | all-gather | bytes 368640 | tf_op jit(solution)/shard_map/all_gather | solution.py:87
  70.3 0.2 copy.116
  70.8 0.5 convolution_convert_fusion.1
  72.0 0.7 fusion.49
  72.8 0.2 fusion.10
  73.3 12.9 %all_gather.7 = bf16[128,1280]{0,1:T(8,128)(2,1)S(1)} all-gather(bf16[128,160]{0,1:T(8,128)(2,1)S(1)} %reshape.223), channel_id=1, replica_groups=mesh['dp'=64,'tensor'=8] {'tensor'}, dimensions={1}, use_global_device_ids=true | all-gather | bytes 368640 | tf_op jit(solution)/shard_map/all_gather | solution.py:87
  86.4 0.4 multiply_reduce_fusion.1
  86.8 10.9 %psum.14 = f32[128]{0:T(128)S(1)} all-reduce(f32[128]{0:T(128)S(1)} %get-tuple-element.58), channel_id=1, replica_groups=mesh['dp'=64,'tensor'=8] {'tensor'}, use_global_device_ids=true, to_apply=%region_11.13 | all-reduce | flops 128 | bytes 1024 | tf_op jit(solution)/shard_map/psum | solution.py:91
  97.8 0.6 gather_fusion.2
  98.5 0.2 fusion.29
  98.7 13.1 %psum.15 = f32[128]{0:T(128)S(1)} all-reduce(f32[128]{0:T(128)S(1)} %get-tuple-element.37), channel_id=1, replica_groups=mesh['dp'=64,'tensor'=8] {'tensor'}, use_global_device_ids=true, to_apply=%region_16.19 | all-reduce | flops 128 | bytes 1024 | tf_op jit(solution)/shard_map/psum | solution.py:91
  112.2 0.8 scatter_custom_fusion
  113.0 0.7 reshape.225
  113.7 15.1 %all-to-all-start.1 = ((bf16[64,2,640]{2,1,0:T(2,128)(2,1)}), bf16[64,2,640]{2,1,0:T(2,128)(2,1)S(1)}, u32[]{:S(2)}, u32[]{:S(2)}) async-start(bf16[64,2,640]{2,1,0:T(2,128)(2,1)} %reshape.225), calls=%async_computation.1 | async-start | bytes 327680 | tf_op jit(solution)/shard_map/all_to_all | solution.py:83
  128.8 0.2 reduce-scatter.2.cloned.1.call-start
  129.0 1.1 convolution_convert_fusion
  130.3 18.1 %all-to-all-done.1 = bf16[64,2,640]{2,1,0:T(2,128)(2,1)S(1)} async-done(((bf16[64,2,640]{2,1,0:T(2,128)(2,1)}), bf16[64,2,640]{2,1,0:T(2,128)(2,1)S(1)}, u32[]{:S(2)}, u32[]{:S(2)}) %all-to-all-start.1) | async-done | bytes 163872 | tf_op jit(solution)/shard_map/all_to_all | solution.py:83
  148.5 0.9 gather_fusion.5
  149.5 0.8 copy.123
  150.3 19.7 %reduce-scatter.2.cloned.1.call-done = bf16[128,160]{0,1:T(8,128)(2,1)} async-done(((bf16[128,1280]{0,1:T(8,128)(2,1)}), bf16[128,160]{0,1:T(8,128)(2,1)}) %reduce-scatter.2.cloned.1.call-update) | async-done | bytes 40976 | tf_op jit(solution)/shard_map/reduce_scatter | solution.py:558
  170.0 0.9 reshape.231
  171.0 0.2 multiply_reduce_fusion
  171.3 0.2 fusion.13
  172.3 78.5 %reduce_gradients.1 = (bf16[1280,480]{1,0:T(8,128)(2,1)S(1)}, bf16[1280,160]{1,0:T(8,128)(2,1)S(1)}, f32[16,128]{1,0:T(8,128)S(1)}) custom-call(bf16[256,1280]{1,0:T(8,128)(2,1)S(1)} %pad_maximum_fusion.lhs_ref, bf16[256,640]{1,0:T(8,128)(2,1)S(1)} %fusion.19.rhs_ref, f32[16,128]{1,0:T(8,128)S(1)} %pad_bitcast_fusion.gain_ref), custom_call_target="tpu_custom_call" | custom-call | tf_op jit(solution)/shard_map/reduce_gradients/pallas_call | solution.py:436
  250.7 0.8 copy-done.1
  251.6 1.5 copy.131
  253.0 1.0 copy.132
  254.0 0.6 slice.52
  (98 shorter events, 5.7 us)
Async XLA Ops:
  7.2 63.7 %copy-start = (bf16[1280,480]{0,1:T(8,128)(2,1)S(1)}, bf16[1280,480]{0,1:T(8,128)(2,1)}, u32[]{:S(2)}) copy-start(bf16[1280,480]{0,1:T(8,128)(2,1)} %param.18) | copy-start | bytes 3686404
  7.2 23.9 %copy-start.6 = (s32[64,64]{1,0:T(8,128)S(1)}, s32[64,64]{1,0:T(8,128)}, u32[]{:S(2)}) copy-start(s32[64,64]{1,0:T(8,128)} %param.14) | copy-start | bytes 49156
  7.2 24.6 %copy-start.8 = (s32[2048,1]{0,1:T(1,128)S(1)}, s32[2048,1]{0,1:T(1,128)}, u32[]{:S(2)}) copy-start(s32[2048,1]{0,1:T(1,128)} %param.16) | copy-start | bytes 24580
  11.4 25.6 %copy-start.5 = (bf16[128,4,160]{0,2,1:T(8,128)(2,1)S(1)}, bf16[128,4,160]{0,2,1:T(8,128)(2,1)}, u32[]{:S(2)}) copy-start(bf16[128,4,160]{0,2,1:T(8,128)(2,1)} %param.21) | copy-start | bytes 491524
  12.4 36.4 %all-to-all-start = ((bf16[64,4,160]{2,1,0:T(4,128)(2,1)}), bf16[64,4,160]{2,1,0:T(4,128)(2,1)S(1)}, u32[]{:S(2)}, u32[]{:S(2)}) async-start(bf16[64,4,160]{2,1,0:T(4,128)(2,1)} %broadcast_select_fusion.1), calls=%async_computation | async-start | bytes 262144 | tf_op jit(solution)/shard_map/all_to_all | solution.py:83
  37.2 3.9 %copy-start.10 = (s32[2,64]{1,0:T(2,128)S(1)}, s32[2,64]{1,0:T(2,128)}, u32[]{:S(2)}) copy-start(s32[2,64]{1,0:T(2,128)} %param.15) | copy-start | bytes 1540
  48.8 48.9 %all-to-all-start.2 = ((bf16[64,2,640]{2,1,0:T(2,128)(2,1)}), bf16[64,2,640]{2,1,0:T(2,128)(2,1)S(1)}, u32[]{:S(2)}, u32[]{:S(2)}) async-start(bf16[64,2,640]{2,1,0:T(2,128)(2,1)} %reshape.229), calls=%async_computation.2 | async-start | bytes 327680 | tf_op jit(solution)/shard_map/all_to_all | solution.py:83
  56.3 14.4 %copy-start.7 = (f32[1280]{0:T(1024)S(1)}, f32[1280]{0:T(1024)}, u32[]{:S(2)}) copy-start(f32[1280]{0:T(1024)} %param.17) | copy-start | bytes 15364
  72.0 14.4 %copy-start.3 = (bf16[1280,160]{0,1:T(8,128)(2,1)S(1)}, bf16[1280,160]{0,1:T(8,128)(2,1)}, u32[]{:S(2)}) copy-start(bf16[1280,160]{0,1:T(8,128)(2,1)} %param.19) | copy-start | bytes 1228804
  86.2 12.3 %copy-start.9 = (f32[160]{0:T(256)S(1)}, f32[160]{0:T(256)}, u32[]{:S(2)}) copy-start(f32[160]{0:T(256)} %param.20) | copy-start | bytes 1924
  113.7 34.7 %all-to-all-start.1 = ((bf16[64,2,640]{2,1,0:T(2,128)(2,1)}), bf16[64,2,640]{2,1,0:T(2,128)(2,1)S(1)}, u32[]{:S(2)}, u32[]{:S(2)}) async-start(bf16[64,2,640]{2,1,0:T(2,128)(2,1)} %reshape.225), calls=%async_computation.1 | async-start | bytes 327680 | tf_op jit(solution)/shard_map/all_to_all | solution.py:83
  128.8 41.3 %reduce-scatter.2.cloned.1.call-start = ((), (), s32[]{:S(2)}) async-start(), calls=%async_computation.4 | async-start | bytes 368640 | tf_op jit(solution)/shard_map/reduce_scatter | solution.py:558
  148.5 22.5 %copy-start.4 = (f32[2,2,64,64]{2,3,1,0:T(8,128)S(1)}, f32[2,2,64,64]{2,3,1,0:T(8,128)}, u32[]{:S(2)}) copy-start(f32[2,2,64,64]{2,3,1,0:T(8,128)} %get-tuple-element.57) | copy-start | bytes 196612
  250.7 0.8 copy-start.1
  251.6 1.5 copy-start.2
Sparse Core Ops, SparseCore 0:
  133.0 37.0 reduce-scatter.1

commit v2 on v1

v2 whole, which is shorter than its diff:
```python
import functools
import math

import jax
import jax.numpy as jnp
from jax import lax
from jax.experimental import pallas as pl
from jax.experimental.pallas import tpu as pltpu
from jax.sharding import PartitionSpec as P

HD = 80
WIN = 64
EPS = 1e-06
NY = 4
MESH = pl.DeviceIdType.MESH


def copy(src, dst, ss, rs, peer):
    return pltpu.make_async_remote_copy(
        src_ref=src, dst_ref=dst, send_sem=ss, recv_sem=rs, device_id=peer, device_id_type=MESH
    )


def iota(shape, dim):
    return lax.broadcasted_iota(jnp.int32, shape, dim)


def pick(cond):
    return jnp.where(cond, 1.0, 0.0).astype(jnp.bfloat16)


def to_row(col):
    n = col.shape[0]
    return jnp.sum(jnp.where(iota((n, n), 0) == iota((n, n), 1), col, 0.0), axis=0, keepdims=True)


def to_col(row):
    n = row.shape[1]
    return jnp.sum(jnp.where(iota((n, n), 0) == iota((n, n), 1), row, 0.0), axis=1, keepdims=True)


def dot(a, b, ca=1, cb=0):
    return lax.dot_general(a, b, (((ca,), (cb,)), ((), ())), preferred_element_type=jnp.float32)


def sum_chunks(
    nz,
    ny,
    me,
    z,
    y,
    dev,
    meanwhile,
    lhs_ref,
    rhs_ref,
    gain_ref,
    qkv_ref,
    out_ref,
    gsum_ref,
    part,
    full,
    c_buf,
    n_buf,
    p_buf,
    zs_up,
    zs_dn,
    zr_up,
    zr_dn,
    y_ss,
    y_rs,
    z_ss,
    z_rs,
    g_ss,
    g_rs,
    f_ss,
    f_rs,
):
    up_y, dn_y, up_z, dn_z = dev(z, y + 1), dev(z, y - 1), dev(z + 1, y), dev(z - 1, y)
    half = nz // 2
    width, cols = lhs_ref.shape[0], rhs_ref.shape[0]
    per_row = cols // 128
    live = (width // 16) * per_row
    tiles = part.shape[0]
    per = tiles // (nz * ny)
    block = 160
    per_block = (block // 16) * per_row

    def products(b, carry):
        got = lax.dot_general(
            lhs_ref[pl.ds(pl.multiple_of(b * block, block), block), :],
            rhs_ref[...],
            (((1,), (1,)), ((), ())),
            preferred_element_type=jnp.float32,
        ).astype(jnp.bfloat16)
        for i in range(block // 16):
            for c in range(per_row):
                part[b * per_block + i * per_row + c] = got[16 * i : 16 * i + 16, 128 * c : 128 * c + 128]
        return carry

    lax.fori_loop(0, width // block, products, 0)
    part[pl.ds(live, tiles - live)] = jnp.zeros((tiles - live, 16, 128), jnp.bfloat16)
    part[live] = gain_ref[...].astype(jnp.bfloat16)

    def spot(yy, d):
        return pl.ds((lax.rem(yy + ny, ny) * nz + d) * per, per)

    def c_copy(d, fwd):
        src = part.at[spot(y + 2, d)]
        return copy(src, c_buf.at[d], y_ss.at[0, d], y_rs.at[0, d], up_y if fwd else dn_y)

    def n_copy(d, fwd):
        src = part.at[spot(y - 1 if fwd else y + 1, d)]
        return copy(src, n_buf.at[d], y_ss.at[1, d], y_rs.at[1, d], dn_y if fwd else up_y)

    def p_copy(d, fwd):
        src = part.at[spot(y + 1 if fwd else y - 1, d)]
        return copy(src, p_buf.at[d], y_ss.at[2, d], y_rs.at[2, d], up_y if fwd else dn_y)

    def both(d, act):
        even = lax.rem(d, 2) == 0

        @pl.when(even)
        def _():
            act(True)

        @pl.when(jnp.logical_not(even))
        def _():
            act(False)

    def y_first(d):
        def act(fwd):
            c_copy(d, fwd).start()
            n_copy(d, fwd).start()

        both(d, act)

    def y_second(d):
        def act(fwd):
            c_copy(d, fwd).wait_recv()
            here = spot(y + 1 if fwd else y - 1, d)
            total = part[here].astype(jnp.float32) + c_buf[d].astype(jnp.float32)
            part[here] = total.astype(jnp.bfloat16)
            p_copy(d, fwd).start()

        both(d, act)

    def y_sum(d):
        n_copy(d, True).wait_recv()
        p_copy(d, True).wait_recv()
        return (
            part[spot(y, d)].astype(jnp.float32)
            + n_buf[d].astype(jnp.float32)
            + p_buf[d].astype(jnp.float32)
        )

    def up_dest(k):
        return lax.rem(z + half - k, nz)

    def dn_dest(k):
        return lax.rem(z + nz - half + k, nz)

    def group(k, act):
        act(up_dest(k))

        @pl.when(jnp.logical_and(k > 0, k < half))
        def _():
            act(dn_dest(k))

    def zu_copy(k):
        return copy(zs_up.at[k], zr_up.at[k], z_ss.at[0, k], z_rs.at[0, k], up_z)

    def zd_copy(k):
        return copy(zs_dn.at[k], zr_dn.at[k], z_ss.at[1, k], z_rs.at[1, k], dn_z)

    ahead_first, ahead_second = 3, 1

    def first_group(k, carry):
        group(k, y_first)
        return carry

    def second_group(k, carry):
        group(k, y_second)
        return carry

    lax.fori_loop(0, ahead_first, first_group, 0)
    lax.fori_loop(0, ahead_second, second_group, 0)

    def z_step(k, carry):
        @pl.when(k + ahead_first <= half)
        def _():
            group(k + ahead_first, y_first)

        @pl.when(k + ahead_second <= half)
        def _():
            group(k + ahead_second, y_second)

        @pl.when(k == 0)
        def _():
            zs_up[k] = y_sum(up_dest(k)).astype(jnp.bfloat16)
            zu_copy(k).start()

        @pl.when(k > 0)
        def _():
            total = y_sum(up_dest(k))
            zu_copy(k - 1).wait_recv()
            zs_up[k] = (total + zr_up[k - 1].astype(jnp.float32)).astype(jnp.bfloat16)
            zu_copy(k).start()
            total = y_sum(dn_dest(k))

            @pl.when(k > 1)
            def _():
                zd_copy(k - 1).wait_recv()
                zs_dn[k] = (total + zr_dn[k - 1].astype(jnp.float32)).astype(jnp.bfloat16)

            @pl.when(k == 1)
            def _():
                zs_dn[k] = total.astype(jnp.bfloat16)

            zd_copy(k).start()

        return carry

    lax.fori_loop(0, half, z_step, 0)
    total = y_sum(z)
    zu_copy(half - 1).wait_recv()
    zd_copy(half - 1).wait_recv()
    own = spot(y, z)
    full[own] = (
        total + zr_up[half - 1].astype(jnp.float32) + zr_dn[half - 1].astype(jnp.float32)
    ).astype(jnp.bfloat16)

    def gz_up(s):
        at = full.at[spot(y, lax.rem(z - s + nz, nz))]
        return copy(at, at, g_ss.at[0, s], g_rs.at[0, s], up_z)

    def gz_dn(s):
        at = full.at[spot(y, lax.rem(z + s, nz))]
        return copy(at, at, g_ss.at[1, s], g_rs.at[1, s], dn_z)

    def gz_up_in(s):
        at = full.at[spot(y, lax.rem(z - s - 1 + nz, nz))]
        return copy(at, at, g_ss.at[0, s], g_rs.at[0, s], up_z)

    def gz_dn_in(s):
        at = full.at[spot(y, lax.rem(z + s + 1, nz))]
        return copy(at, at, g_ss.at[1, s], g_rs.at[1, s], dn_z)

    def ya_copy(d, yy):
        at = full.at[spot(yy, d)]
        return copy(at, at, f_ss.at[0, d], f_rs.at[0, d], up_y)

    def yb_copy(d, yy):
        at = full.at[spot(yy, d)]
        return copy(at, at, f_ss.at[1, d], f_rs.at[1, d], dn_y)

    def yf_copy(d, fwd):
        at = full.at[spot(y - 1 if fwd else y + 1, d)]
        return copy(at, at, f_ss.at[2, d], f_rs.at[2, d], up_y if fwd else dn_y)

    def spread(d):
        ya_copy(d, y).start()
        yb_copy(d, y).start()

    def onward(d):
        def act(fwd):
            if fwd:
                ya_copy(d, y - 1).wait_recv()
            else:
                yb_copy(d, y + 1).wait_recv()
            yf_copy(d, fwd).start()

        both(d, act)

    def g_step(s, carry):
        @pl.when(s > 0)
        def _():
            gz_up_in(s - 1).wait_recv()

        gz_up(s).start()

        @pl.when(jnp.logical_and(s > 0, s < half))
        def _():
            gz_dn_in(s - 1).wait_recv()

        @pl.when(s < half - 1)
        def _():
            gz_dn(s).start()

        spread(lax.rem(z - s + nz, nz))

        @pl.when(s > 0)
        def _():
            spread(lax.rem(z + s, nz))

        @pl.when(s > 1)
        def _():
            onward(lax.rem(z - s + 1 + nz, nz))
            onward(lax.rem(z + s - 1, nz))

        @pl.when(s == 1)
        def _():
            onward(z)

        return carry

    lax.fori_loop(0, half, g_step, 0)
    gz_up_in(half - 1).wait_recv()
    spread(lax.rem(z + half, nz))
    onward(lax.rem(z - half + 1 + nz, nz))
    onward(lax.rem(z + half - 1, nz))
    onward(lax.rem(z + half, nz))

    def arrivals(d, carry):
        def act(fwd):
            if fwd:
                yb_copy(d, y + 1).wait_recv()
            else:
                ya_copy(d, y - 1).wait_recv()
            at = full.at[spot(y + 2, d)]
            copy(at, at, f_ss.at[2, d], f_rs.at[2, d], up_y).wait_recv()

        both(d, act)
        return carry

    meanwhile()
    lax.fori_loop(0, nz, arrivals, 0)

    def unpack(r, carry):
        rows = pl.ds(pl.multiple_of(r * 16, 16), 16)
        for c in range(3):
            qkv_ref[rows, 128 * c : 128 * c + 128] = full[r * per_row + c]
        mixed = full[r * per_row + 3]
        qkv_ref[rows, 384:480] = mixed[:, :96]
        out_ref[rows, 128:160] = mixed[:, 96:]
        out_ref[rows, 0:128] = full[r * per_row + 4]
        return carry

    lax.fori_loop(0, width // 16, unpack, 0)
    gsum_ref[...] = full[live].astype(jnp.float32)

    def drain_y(d, carry):
        for j in range(3):
            copy(c_buf.at[d], c_buf.at[d], y_ss.at[j, d], y_rs.at[j, d], up_y).wait_send()
            copy(c_buf.at[d], c_buf.at[d], f_ss.at[j, d], f_rs.at[j, d], up_y).wait_send()
        return carry

    lax.fori_loop(0, nz, drain_y, 0)

    def drain_z(k, carry):
        zu_copy(k).wait_send()
        gz_up(k).wait_send()

        @pl.when(k > 0)
        def _():
            zd_copy(k).wait_send()

        @pl.when(k < half - 1)
        def _():
            gz_dn(k).wait_send()

        return carry

    lax.fori_loop(0, half, drain_z, 0)


def layer_kernel(
    nz,
    ny,
    patches_ref,
    counts_ref,
    ids_ref,
    tok_ref,
    gain1_ref,
    wqkv_ref,
    wout_ref,
    gain2_ref,
    cot_ref,
    merged_ref,
    qkv_ref,
    out_ref,
    gsum_ref,
    row_out,
    row_mid,
    row_in,
    cot_out,
    cot_mid,
    cot_in,
    tok_out,
    tok_mid,
    tok_in,
    x_all,
    attn_all,
    stat_all,
    spread,
    grad_in,
    wqkv_t,
    wout_t,
    gain_col,
    lhs,
    rhs,
    gain_tile,
    hop_ss,
    hop_rs,
    far_ss,
    far_rs,
    t_ss,
    t_rs,
    *reduce_refs,
):
    bf16, f32 = jnp.bfloat16, jnp.float32
    dp = nz * ny
    nt = lax.axis_size("tensor")
    me = lax.axis_index("dp")
    rank = lax.axis_index("tensor")
    z, y = me // ny, lax.rem(me, ny)
    rows_src, features = patches_ref.shape
    rows_own = x_all.shape[1]
    width = x_all.shape[0]
    slot_cap = rows_src // dp
    lm_rows = cot_ref.shape[0]
    token_rows = lm_rows // dp
    token_cap = token_rows // 4
    tokens = rows_own // 4
    heads = wqkv_ref.shape[1] // (3 * HD)
    scaling = 1.0 / math.sqrt(HD)
    log = lambda n: n.bit_length() - 1

    def dev(zz, yy):
        return {"dp": lax.rem(zz + nz, nz) * ny + lax.rem(yy + ny, ny)}

    def mate(i):
        return {"tensor": lax.rem(rank + i, nt)}

    barrier = pltpu.get_barrier_semaphore()
    for i in range(1, ny):
        pl.semaphore_signal(barrier, inc=1, device_id=dev(z, y + i), device_id_type=MESH)
    for i in range(1, nt):
        pl.semaphore_signal(barrier, inc=1, device_id=mate(i), device_id_type=MESH)
    for i in range(1, nz):
        pl.semaphore_signal(barrier, inc=1, device_id=dev(z + i, y), device_id_type=MESH)

    def owner_of(shape, dim, per):
        at = iota(shape, dim) >> log(per)
        return (at & (nz - 1)) * ny + (at >> log(nz))

    def hop(k, out, mid, i):
        to = lax.rem(y + i, ny)
        return copy(out.at[to], mid.at[y], hop_ss.at[k, i - 1], hop_rs.at[k, i - 1], dev(z, y + i))

    def far(k, mid, got, i):
        to = lax.rem(z + i, nz)
        return copy(
            mid.at[:, to], got.at[z], far_ss.at[k, i - 1], far_rs.at[k, i - 1], dev(z + i, y)
        )

    def first_hop(k, out, mid):
        for i in range(1, ny):
            hop(k, out, mid, i).start()
        mid[y] = out[y]

    def second_hop(k, out, mid, got):
        for i in range(1, ny):
            hop(k, out, mid, i).wait_recv()

        def send(i, carry):
            far(k, mid, got, i).start()
            return carry

        lax.fori_loop(1, nz, send, 0)
        got[z] = mid[:, z]

    def landed(k, mid, got):
        def take(i, carry):
            far(k, mid, got, i).wait_recv()
            return carry

        lax.fori_loop(1, nz, take, 0)

    n = rows_src
    own_row = counts_ref[pl.ds(me, 1), :].astype(f32)
    start = jnp.sum(
        jnp.where(iota((n, dp), 1) < owner_of((n, dp), 0, slot_cap), own_row, 0.0),
        axis=1,
        keepdims=True,
    ).astype(jnp.int32)
    slot = iota((n, 1), 0) & (slot_cap - 1)
    chosen = pick(iota((n, rows_src), 1) == jnp.minimum(start + slot, rows_src - 1))
    row_out[...] = dot(chosen, patches_ref[...]).reshape(row_out.shape).astype(bf16)

    pl.semaphore_wait(barrier, ny - 1 + nt - 1 + nz - 1)
    first_hop(0, row_out, row_mid)

    tok = tok_ref[...]
    lm_col = jnp.sum(jnp.where(tok == me, 1.0, 0.0), axis=1, keepdims=True)
    lm_row = to_row(lm_col)
    n = lm_rows
    start = jnp.sum(
        jnp.where(iota((n, dp), 1) < owner_of((n, dp), 0, token_rows), lm_row, 0.0),
        axis=1,
        keepdims=True,
    ).astype(jnp.int32)
    slot = (iota((n, 1), 0) & (token_rows - 1)) >> 2
    quarter = iota((n, 1), 0) & 3
    place = jnp.minimum(start + slot, lm_rows // 4 - 1) * 4 + quarter
    chosen = pick(iota((n, n), 1) == place)
    cot_out[...] = dot(chosen, cot_ref[...]).reshape(cot_out.shape).astype(bf16)

    second_hop(0, row_out, row_mid, row_in)
    first_hop(1, cot_out, cot_mid)

    n = rows_src
    sent_col = jnp.sum(
        jnp.where(iota((dp, dp), 1) == me, counts_ref[...].astype(f32), 0.0), axis=1, keepdims=True
    )
    sent_row = to_row(sent_col)
    source = iota((n, dp), 0) >> log(slot_cap)
    start = jnp.sum(jnp.where(iota((n, dp), 1) < source, sent_row, 0.0), axis=1, keepdims=True)
    count = jnp.sum(jnp.where(iota((n, dp), 1) == source, sent_row, 0.0), axis=1, keepdims=True)
    slot = iota((n, 1), 0) & (slot_cap - 1)
    where_to = jnp.where(slot < count.astype(jnp.int32), start.astype(jnp.int32) + slot, -1)
    placed = pick(iota((n, rows_own), 1) == where_to)

    wqkv_t[...] = wqkv_ref[...].T
    second_hop(1, cot_out, cot_mid, cot_in)

    landed(0, row_mid, row_in)
    own = pl.ds(pl.multiple_of(rank * features, 16), features)
    arrived = row_in[...].astype(f32).reshape(rows_src, features).astype(bf16)
    x_own = dot(arrived, placed, 0, 0)
    x_all[own, :] = x_own.astype(bf16)

    def gather(k, buf, i):
        return copy(buf.at[own, :], buf.at[own, :], t_ss.at[k, i - 1], t_rs.at[k, i - 1], mate(i))

    for i in range(1, nt):
        gather(0, x_all, i).start()

    wout_t[...] = wout_ref[...].T
    for b in range(width // 160):
        gain_col[160 * b : 160 * b + 160, :] = to_col(gain1_ref[:, 160 * b : 160 * b + 160])
    merge_gain = to_col(gain2_ref[...])
    ids_row = ids_ref[...].astype(f32)
    same = to_col(ids_row) == ids_row

    target = tok_ref[pl.ds(me, 1), :].astype(f32)
    target_col = to_col(target)
    before = iota((tokens, tokens), 0) < iota((tokens, tokens), 1)
    order = jnp.sum(
        jnp.where(jnp.logical_and(target_col == target, before), 1.0, 0.0), axis=0, keepdims=True
    )
    token_slot = to_col(target * token_rows + order * 4)
    of_row = iota((tokens, rows_own), 1) >> 2
    slot_row = jnp.sum(
        jnp.where(iota((tokens, rows_own), 0) == of_row, token_slot, 0.0), axis=0, keepdims=True
    ).astype(jnp.int32) + (iota((1, rows_own), 1) & 3)
    taken = pick(iota((lm_rows, rows_own), 0) == slot_row)
    sent_id = owner_of((lm_rows, rows_own), 0, token_rows) * token_rows + (
        iota((lm_rows, rows_own), 0) & (token_rows - 1)
    )
    given = pick(sent_id == slot_row)

    for i in range(1, nt):
        gather(0, x_all, i).wait_recv()
    x = x_all[...].astype(f32)
    inv_first = lax.rsqrt(jnp.sum(x * x, axis=0, keepdims=True) / width + EPS)
    normed_in = (x * inv_first * gain_col[...]).astype(bf16)
    lhs[:, 0:rows_own] = normed_in
    packed = dot(wqkv_t[...], normed_in).astype(bf16)

    kept = []
    for h in range(heads):
        q, k, v = (packed[(3 * h + s) * HD : (3 * h + s + 1) * HD] for s in range(3))
        scores = jnp.where(same, dot(k, q, 0, 0) * scaling, -jnp.inf)
        raised = jnp.exp(scores - jnp.max(scores, axis=0, keepdims=True))
        weights = raised / jnp.sum(raised, axis=0, keepdims=True)
        rounded = weights.astype(bf16)
        at = pl.ds(pl.multiple_of(rank * features + h * HD, 16), HD)
        attn_all[at, :] = dot(v, rounded).astype(bf16)
        kept.append((q, k, v, weights, rounded))

    for i in range(1, nt):
        gather(1, attn_all, i).start()
    landed(1, cot_mid, cot_in)
    returned = cot_in[...].astype(f32).reshape(lm_rows, features).astype(bf16)
    upstream = dot(returned, taken, 0, 0)
    for i in range(1, nt):
        gather(1, attn_all, i).wait_recv()

    attn = attn_all[...]
    lhs[:, rows_own : 2 * rows_own] = attn
    residual = x_own + dot(wout_t[...], attn)
    lifted = merge_gain * upstream
    sums = [
        jnp.sum(residual * residual, axis=0, keepdims=True),
        jnp.sum(lifted * residual, axis=0, keepdims=True),
    ]
    stat_all[rank] = jnp.concatenate(sums + [jnp.zeros((6, rows_own), f32)], axis=0)

    def stat(i):
        at = stat_all.at[rank]
        return copy(at, at, t_ss.at[2, i - 1], t_rs.at[2, i - 1], mate(i))

    for i in range(1, nt):
        stat(i).start()
    for i in range(1, nt):
        stat(i).wait_recv()
    stats = jnp.sum(stat_all[...], axis=0)
    inv_second = lax.rsqrt(stats[0:1] / width + EPS)
    along = stats[1:2]
    scaled = residual * inv_second
    dresidual = (
        lifted * inv_second - residual * (along * (inv_second * inv_second * inv_second) / width)
    ).astype(bf16)
    spread[...] = dot(wout_ref[...], dresidual).astype(bf16)

    def share(i):
        to = lax.rem(rank + i, nt)
        src = spread.at[pl.ds(pl.multiple_of(to * features, 16), features), :]
        return copy(src, grad_in.at[rank], t_ss.at[3, i - 1], t_rs.at[3, i - 1], mate(i))

    for i in range(1, nt):
        share(i).start()
    grad_in[rank] = spread[own, :]

    normed = (scaled * merge_gain).astype(bf16)
    tok_out[...] = dot(given, normed, 1, 1).reshape(tok_out.shape).astype(bf16)
    first_hop(2, tok_out, tok_mid)

    gains = jnp.sum(upstream * scaled, axis=1, keepdims=True)
    lane, sub = iota((features, 128), 1), iota((features, 128), 0)
    head = jnp.sum(jnp.where(lane == sub, gains, 0.0), axis=0, keepdims=True)
    tail = jnp.sum(jnp.where(lane + 128 == sub, gains, 0.0), axis=0, keepdims=True)
    gain_tile[...] = jnp.concatenate([head, tail, jnp.zeros((14, 128), f32)], axis=0)

    base = 3 * heads * HD
    rhs[0:base, rows_own : 2 * rows_own] = jnp.zeros((base, rows_own), bf16)
    rhs[base : base + features, 0:rows_own] = jnp.zeros((features, rows_own), bf16)
    rhs[base : base + features - 128, rows_own : 2 * rows_own] = dresidual[128:]
    rhs[base + features - 128 : base + features, rows_own : 2 * rows_own] = dresidual[:128]

    second_hop(2, tok_out, tok_mid, tok_in)
    for i in range(1, nt):
        share(i).wait_recv()
    total = grad_in[0].astype(f32)
    for r in range(1, nt):
        total = total + grad_in[r].astype(f32)
    attn_grad = total.astype(bf16)

    for h in range(heads):
        q, k, v, weights, rounded = kept[h]
        g = attn_grad[h * HD : (h + 1) * HD]
        dprobs = dot(v, g, 0, 0)
        row_dot = jnp.sum(weights * dprobs, axis=0, keepdims=True)
        dscores = (weights * (dprobs - row_dot)).astype(bf16)
        at = 3 * h * HD
        rhs[at : at + HD, 0:rows_own] = (dot(k, dscores) * scaling).astype(bf16)
        rhs[at + HD : at + 2 * HD, 0:rows_own] = (dot(q, dscores, 1, 1) * scaling).astype(bf16)
        rhs[at + 2 * HD : at + 3 * HD, 0:rows_own] = dot(g, rounded, 1, 1).astype(bf16)

    def place_tokens():
        landed(2, tok_mid, tok_in)
        n = lm_rows
        owner = iota((dp, n), 1) >> log(token_rows)
        start = jnp.sum(jnp.where(iota((dp, n), 0) < owner, lm_col, 0.0), axis=0, keepdims=True)
        count = jnp.sum(jnp.where(iota((dp, n), 0) == owner, lm_col, 0.0), axis=0, keepdims=True)
        slot = (iota((1, n), 1) & (token_rows - 1)) >> 2
        to = (start.astype(jnp.int32) + slot) * 4 + (iota((1, n), 1) & 3)
        to = jnp.where(slot < count.astype(jnp.int32), to, -1)
        put = pick(iota((n, n), 0) == to)
        got = tok_in[...].astype(f32).reshape(n, features).astype(bf16)
        merged_ref[...] = dot(put, got).astype(bf16)

    sum_chunks(
        nz,
        ny,
        me,
        z,
        y,
        dev,
        place_tokens,
        lhs,
        rhs,
        gain_tile,
        qkv_ref,
        out_ref,
        gsum_ref,
        *reduce_refs,
    )

    for k, (out, mid, got) in enumerate(
        ((row_out, row_mid, row_in), (cot_out, cot_mid, cot_in), (tok_out, tok_mid, tok_in))
    ):
        for i in range(1, ny):
            hop(k, out, mid, i).wait_send()

        def drain(i, carry, k=k, mid=mid, got=got):
            far(k, mid, got, i).wait_send()
            return carry

        lax.fori_loop(1, nz, drain, 0)
    for i in range(1, nt):
        gather(0, x_all, i).wait_send()
        gather(1, attn_all, i).wait_send()
        stat(i).wait_send()
        share(i).wait_send()


def body(
    patches,
    send_counts,
    window_ids,
    token_shard,
    first_gain,
    qkv_weight,
    out_weight,
    merge_gain,
    cotangent,
):
    bf16, f32 = jnp.bfloat16, jnp.float32
    dp, nt = lax.axis_size("dp"), lax.axis_size("tensor")
    ny = NY
    nz = dp // ny
    half = nz // 2
    rows_src, features = patches.shape
    rows_own = rows_src // 2
    lm_slots = cotangent.shape[0]
    lm_rows = 4 * lm_slots
    width = first_gain.shape[0]
    packed = qkv_weight.shape[1]
    cols = packed + features
    live = (width // 16) * (cols // 128)
    per = -(-(live + 1) // dp)
    tiles = window_ids.shape[0]
    ids = (window_ids + 4 * jnp.arange(tiles, dtype=jnp.int32)[:, None]).reshape(1, rows_own)
    vmem = pl.BlockSpec(memory_space=pltpu.VMEM)
    sems = pltpu.SemaphoreType.DMA

    def held(*shape, dtype=bf16):
        return pltpu.VMEM(shape, dtype)

    def legs(rows):
        out = held(ny, nz, rows, features)
        return [out, out, held(nz, ny, rows, features)]

    merged, qkv_grad, out_grad, gain_sum = pl.pallas_call(
        functools.partial(layer_kernel, nz, ny),
        out_shape=(
            jax.ShapeDtypeStruct((lm_rows, features), bf16),
            jax.ShapeDtypeStruct((width, packed), bf16),
            jax.ShapeDtypeStruct((width, features), bf16),
            jax.ShapeDtypeStruct((16, 128), f32),
        ),
        in_specs=[vmem] * 9,
        out_specs=(vmem,) * 4,
        scratch_shapes=[
            *legs(rows_src // dp),
            *legs(lm_rows // dp),
            *legs(lm_rows // dp),
            held(width, rows_own),
            held(width, rows_own),
            held(nt, 8, rows_own, dtype=f32),
            held(width, rows_own),
            held(nt, features, rows_own),
            held(packed, width),
            held(features, width),
            held(width, 1, dtype=f32),
            held(width, 2 * rows_own),
            held(cols, 2 * rows_own),
            held(16, 128, dtype=f32),
            sems((3, ny - 1)),
            sems((3, ny - 1)),
            sems((3, nz - 1)),
            sems((3, nz - 1)),
            sems((4, nt - 1)),
            sems((4, nt - 1)),
            held(per * dp, 16, 128),
            held(per * dp, 16, 128),
            held(nz, per, 16, 128),
            held(nz, per, 16, 128),
            held(nz, per, 16, 128),
            held(half, per, 16, 128),
            held(half, per, 16, 128),
            held(half, per, 16, 128),
            held(half, per, 16, 128),
            sems((3, nz)),
            sems((3, nz)),
            sems((2, half)),
            sems((2, half)),
            sems((2, half)),
            sems((2, half)),
            sems((3, nz)),
            sems((3, nz)),
        ],
        compiler_params=pltpu.CompilerParams(
            collective_id=0, has_side_effects=True, vmem_limit_bytes=56 * 1024 * 1024
        ),
        name="layer",
    )(
        patches,
        send_counts,
        ids,
        token_shard.reshape(dp, rows_own // 4),
        first_gain.reshape(1, width),
        qkv_weight,
        out_weight,
        merge_gain.reshape(1, features),
        cotangent.reshape(lm_rows, features),
    )
    return (
        merged.reshape(lm_slots, 4, features),
        qkv_grad,
        out_grad,
        gain_sum.reshape(-1)[:features],
    )


def solution(mesh):
    placed = (
        P("dp", "tensor"),
        P(),
        P("dp", None),
        P(),
        P(),
        P(None, "tensor"),
        P(None, "tensor"),
        P("tensor"),
        P("dp", None, "tensor"),
    )
    return jax.shard_map(
        body,
        mesh=mesh,
        in_specs=placed,
        out_specs=(P("dp", None, "tensor"), P(None, "tensor"), P(None, "tensor"), P("tensor")),
        check_vma=False,
    )
```

time: 265 us -> 151 us (0.57)
  Pallas kernels: 78.5 us -> 130 us
  blocking collectives: 49.9 us -> 0 us
  waiting for transfers between devices: 45.5 us -> 0 us
  starting transfers between devices: 41.5 us -> 0 us
  between operations: 14.6 us -> 0.69 us
  other arithmetic: 8.32 us -> 2.24 us
  local copies, waits for them, and re-layouts: 20.1 us -> 16 us
  matrix products: 3.08 us -> 0 us
    pallas_call x1, Pallas kernels: 78.5 us -> 130 us  [body(): pl.pallas_call(functools.partial(layer_kernel, nz, ny), out_shape=(jax.Sh...]
    all_to_all x3 -> x0, starting transfers between devices: 41.3 us -> none  [ragged(): lax.all_to_all(buffers, 'dp', split_axis=0, concat_axis=0, tiled=True)]
    all_gather x2 -> x0, blocking collectives: 25.8 us -> none  [full_rows(): return lax.all_gather(shard_part, 'tensor', axis=1, tiled=True)]
    all_to_all x3 -> x0, waiting for transfers between devices: 25.7 us -> none  [ragged(): lax.all_to_all(buffers, 'dp', split_axis=0, concat_axis=0, tiled=True)]
    psum x2 -> x0, blocking collectives: 24.1 us -> none  [row_total(): return lax.psum(values, 'tensor')]
    reduce_scatter x1 -> x0, waiting for transfers between devices: 19.7 us -> none  [body(): lax.psum_scatter(spread.astype(jnp.bfloat16), 'tensor', scatter_dimension...]
    gather x9 -> x0, local copies, waits for them, and re-layouts: 7.02 us -> none  [the longest x2 2.45 us: locate(): offset = position - jnp.take(starts, source)]
    unnamed x29 -> x14, local copies, waits for them, and re-layouts: 5.13 us -> 10.2 us
  transfers between devices with their start and end apart: 4 -> 0, of which waited for: 3 -> 0; matrix products, arithmetic and copies ran while one was open for 7% -> 0% of each run, Pallas kernels for 0% -> 0%
where the time goes in v2:
time: 151 us; the launch traced here: 149 us
  Pallas kernels  130 us (86%)
  local copies, waits for them, and re-layouts  16 us (11%)
  other arithmetic  2.24 us (1%)
    pallas_call x1, Pallas kernels, body(): pl.pallas_call(functools.partial(layer_kernel, nz, ny), out_shape=(jax.Sh...  130 us
    unnamed x14, local copies, waits for them, and re-layouts  10.2 us

profile of v2, /device:TPU:6, one launch (start us, length us, event | category | flops | bytes accessed | tf_op | source)
XLA Modules:
  0.0 149.0 jit_solution(17255436918591045802)
XLA Ops:
  0.6 0.0 copy-start.2
  0.6 0.0 copy-start.1
  0.7 0.9 broadcast_add_fusion
  1.5 0.6 reshape.34.ids_ref
  2.1 1.3 reshape.36.gain1_ref
  3.4 0.5 broadcast.13
  3.9 1.4 reduce.3
  5.3 0.7 reshape.35.tok_ref
  6.0 1.6 %copy.21.patches_ref = bf16[256,160]{1,0:T(8,128)(2,1)} copy(bf16[256,160]{0,1:T(8,128)(2,1)} %param.9) | data formatting | bytes 163840 | tf_op args[0]
  7.6 1.1 copy.20
  8.7 0.9 reshape.38.cot_ref
  9.6 0.0 copy-done.2
  9.6 1.1 copy.23.wout_ref
  10.7 0.0 copy-done.1
  10.7 1.5 copy.22.wqkv_ref
  12.1 130.1 %layer.1 = (bf16[512,160]{1,0:T(8,128)(2,1)}, bf16[1280,480]{1,0:T(8,128)(2,1)}, bf16[1280,160]{1,0:T(8,128)(2,1)}, f32[16,128]{1,0:T(8,128)}) custom-call(bf16[256,160]{1,0:T(8,128)(2,1)} %copy.21.patches_ref, s32[64,64]{1,0:T(8,128)} %counts_ref.1, s32[1,128]{1,0:T(1,128)} %reshape.34.ids_ref, s32[64,32]{1,0:T(8,128)} %reshape.35.tok_ref, ...), custom_call_target="tpu_custom_call" | custom-call | tf_op jit(solution)/shard_map/layer/pallas_call | solution.py:745
  142.2 0.0 copy-start
  142.2 1.1 reshape.39
  143.4 0.9 copy.24
  144.2 1.2 slice.4
  145.5 2.1 %copy.26 = bf16[1280,160]{0,1:T(8,128)(2,1)} copy(bf16[1280,160]{1,0:T(8,128)(2,1)} %get-tuple-element.18) | data formatting | bytes 819200
  147.5 0.0 copy-done
  147.5 1.5 copy.25
  (1 shorter events, 0.0 us)
Async XLA Ops:
  0.6 9.0 %copy-start.2 = (bf16[1280,160]{0,1:T(8,128)(2,1)S(1)}, bf16[1280,160]{0,1:T(8,128)(2,1)}, u32[]{:S(2)}) copy-start(bf16[1280,160]{0,1:T(8,128)(2,1)} %param.15) | copy-start | bytes 1228804
  0.6 10.0 %copy-start.1 = (bf16[1280,480]{0,1:T(8,128)(2,1)S(1)}, bf16[1280,480]{0,1:T(8,128)(2,1)}, u32[]{:S(2)}) copy-start(bf16[1280,480]{0,1:T(8,128)(2,1)} %param.14) | copy-start | bytes 3686404
  142.2 5.3 %copy-start = (bf16[1280,480]{1,0:T(8,128)(2,1)S(1)}, bf16[1280,480]{1,0:T(8,128)(2,1)}, u32[]{:S(2)}) copy-start(bf16[1280,480]{1,0:T(8,128)(2,1)} %get-tuple-element.17) | copy-start | bytes 3686404

commit v3 on v2

v3 whole, which is shorter than its diff:
```python
import functools
import math

import jax
import jax.numpy as jnp
from jax import lax
from jax.experimental import pallas as pl
from jax.experimental.pallas import tpu as pltpu
from jax.sharding import PartitionSpec as P

HD = 80
WIN = 64
EPS = 1e-06
NY = 4
MESH = pl.DeviceIdType.MESH


def copy(src, dst, ss, rs, peer):
    return pltpu.make_async_remote_copy(
        src_ref=src, dst_ref=dst, send_sem=ss, recv_sem=rs, device_id=peer, device_id_type=MESH
    )


def iota(shape, dim):
    return lax.broadcasted_iota(jnp.int32, shape, dim)


def pick(cond):
    return jnp.where(cond, 1.0, 0.0).astype(jnp.bfloat16)


def to_row(col):
    n = col.shape[0]
    return jnp.sum(jnp.where(iota((n, n), 0) == iota((n, n), 1), col, 0.0), axis=0, keepdims=True)


def to_col(row):
    n = row.shape[1]
    return jnp.sum(jnp.where(iota((n, n), 0) == iota((n, n), 1), row, 0.0), axis=1, keepdims=True)


def dot(a, b, ca=1, cb=0):
    return lax.dot_general(a, b, (((ca,), (cb,)), ((), ())), preferred_element_type=jnp.float32)


def layer_kernel(
    nz,
    ny,
    patches_ref,
    counts_ref,
    ids_ref,
    tok_ref,
    gain1_ref,
    wqkv_t,
    wout_t,
    gain2_ref,
    cot_ref,
    merged_ref,
    qkv_ref,
    out_ref,
    gsum_ref,
    row_out,
    row_mid,
    row_in,
    cot_out,
    cot_mid,
    cot_in,
    tok_out,
    tok_mid,
    tok_in,
    x_all,
    attn_all,
    stat_all,
    spread,
    grad_in,
    wout,
    gain_col,
    lhs,
    lhs_in,
    rhs,
    rhs_in,
    part,
    near_in,
    class_sum,
    apart_in,
    full,
    hop_ss,
    hop_rs,
    far_ss,
    far_rs,
    t_ss,
    t_rs,
    y_ss,
    y_rs,
    z_ss,
    z_rs,
    g_ss,
    g_rs,
):
    bf16, f32 = jnp.bfloat16, jnp.float32
    dp = nz * ny
    nt = lax.axis_size("tensor")
    me = lax.axis_index("dp")
    rank = lax.axis_index("tensor")
    z, y = me // ny, lax.rem(me, ny)
    features, rows_src = patches_ref.shape
    rows_own = x_all.shape[1]
    width = x_all.shape[0]
    slot_cap = rows_src // dp
    lm_rows = 4 * cot_ref.shape[2]
    token_rows = lm_rows // dp
    token_cap = token_rows // 4
    tokens = rows_own // 4
    heads = wqkv_t.shape[0] // (3 * HD)
    groups = nz // 4
    scaling = 1.0 / math.sqrt(HD)
    log = lambda n: n.bit_length() - 1

    def dev(zz, yy):
        return {"dp": lax.rem(zz + nz, nz) * ny + lax.rem(yy + ny, ny)}

    def mate(i):
        return {"tensor": lax.rem(rank + i, nt)}

    barrier = pltpu.get_barrier_semaphore()
    for i in range(1, ny):
        pl.semaphore_signal(barrier, inc=1, device_id=dev(z, y + i), device_id_type=MESH)
    for i in range(1, nt):
        pl.semaphore_signal(barrier, inc=1, device_id=mate(i), device_id_type=MESH)
    for i in range(1, nz):
        pl.semaphore_signal(barrier, inc=1, device_id=dev(z + i, y), device_id_type=MESH)

    def owner_of(shape, dim, per):
        at = iota(shape, dim) >> log(per)
        return (at & (nz - 1)) * ny + (at >> log(nz))

    def hop(k, out, mid, i):
        to = lax.rem(y + i, ny)
        return copy(out.at[to], mid.at[y], hop_ss.at[k, i - 1], hop_rs.at[k, i - 1], dev(z, y + i))

    def far(k, mid, got, i):
        to = lax.rem(z + i, nz)
        return copy(
            mid.at[:, to], got.at[z], far_ss.at[k, i - 1], far_rs.at[k, i - 1], dev(z + i, y)
        )

    def first_hop(k, out, mid):
        for i in range(1, ny):
            hop(k, out, mid, i).start()
        mid[y] = out[y]

    def second_hop(k, out, mid, got):
        for i in range(1, ny):
            hop(k, out, mid, i).wait_recv()

        def send(i, carry):
            far(k, mid, got, i).start()
            return carry

        lax.fori_loop(1, nz, send, 0)
        got[z] = mid[:, z]

    def landed(k, mid, got):
        def take(i, carry):
            far(k, mid, got, i).wait_recv()
            return carry

        lax.fori_loop(1, nz, take, 0)

    n = rows_src
    own_row = counts_ref[pl.ds(me, 1), :].astype(f32)
    start = jnp.sum(
        jnp.where(iota((n, dp), 1) < owner_of((n, dp), 0, slot_cap), own_row, 0.0),
        axis=1,
        keepdims=True,
    ).astype(jnp.int32)
    slot = iota((n, 1), 0) & (slot_cap - 1)
    chosen = pick(iota((n, rows_src), 1) == jnp.minimum(start + slot, rows_src - 1))
    row_out[...] = dot(chosen, patches_ref[...], 1, 1).reshape(row_out.shape).astype(bf16)

    pl.semaphore_wait(barrier, ny - 1 + nt - 1 + nz - 1)
    first_hop(0, row_out, row_mid)

    lines = tok_ref.shape[1] // 128
    tok = jnp.concatenate([tok_ref[:, 128 * a : 128 * a + 128] for a in range(lines)], axis=0)
    tok = tok.astype(f32)
    per_line = log(128 // tokens)
    line = pick(iota((dp, lines), 1) == iota((dp, lines), 0) >> per_line)
    tok = dot(line, tok.astype(bf16))
    mine = (iota((dp, 128), 1) >> log(tokens)) == (iota((dp, 128), 0) & (128 // tokens - 1))
    named = jnp.logical_and(mine, tok == me.astype(f32))
    lm_row = to_row(jnp.sum(jnp.where(named, 1.0, 0.0), axis=1, keepdims=True))
    n = lm_rows
    start = jnp.sum(
        jnp.where(iota((n, dp), 1) < owner_of((n, dp), 0, token_rows), lm_row, 0.0),
        axis=1,
        keepdims=True,
    ).astype(jnp.int32)
    slot = (iota((n, 1), 0) & (token_rows - 1)) >> 2
    quarter = iota((n, 1), 0) & 3
    place = jnp.minimum(start + slot, lm_rows // 4 - 1)
    total = jnp.zeros((n, features), f32)
    for quart in range(4):
        place_q = jnp.where(quarter == quart, place, -1)
        total = total + dot(pick(iota((n, lm_rows // 4), 1) == place_q), cot_ref[quart], 1, 1)
    cot_out[...] = total.reshape(cot_out.shape).astype(bf16)

    second_hop(0, row_out, row_mid, row_in)
    first_hop(1, cot_out, cot_mid)

    n = rows_src
    sent_col = jnp.sum(
        jnp.where(iota((dp, dp), 1) == me, counts_ref[...].astype(f32), 0.0), axis=1, keepdims=True
    )
    sent_row = to_row(sent_col)
    source = iota((n, dp), 0) >> log(slot_cap)
    start = jnp.sum(jnp.where(iota((n, dp), 1) < source, sent_row, 0.0), axis=1, keepdims=True)
    count = jnp.sum(jnp.where(iota((n, dp), 1) == source, sent_row, 0.0), axis=1, keepdims=True)
    slot = iota((n, 1), 0) & (slot_cap - 1)
    where_to = jnp.where(slot < count.astype(jnp.int32), start.astype(jnp.int32) + slot, -1)
    placed = pick(iota((n, rows_own), 1) == where_to)

    second_hop(1, cot_out, cot_mid, cot_in)

    landed(0, row_mid, row_in)
    own = pl.ds(pl.multiple_of(rank * features, 16), features)
    arrived = row_in[...].astype(f32).reshape(rows_src, features).astype(bf16)
    x_own = dot(arrived, placed, 0, 0)
    x_all[own, :] = x_own.astype(bf16)

    def gather(k, buf, i):
        return copy(buf.at[own, :], buf.at[own, :], t_ss.at[k, i - 1], t_rs.at[k, i - 1], mate(i))

    for i in range(1, nt):
        gather(0, x_all, i).start()

    wout[...] = wout_t[...].T
    for b in range(width // 128):
        gain_col[128 * b : 128 * b + 128, :] = to_col(
            gain1_ref[128 * b : 128 * b + 128].reshape(1, 128)
        )
    merge_gain = to_col(gain2_ref[...])
    ids_col = jnp.concatenate(
        [to_col(ids_ref[a : a + 1, :].astype(f32)) + 4.0 * a for a in range(rows_own // WIN)], axis=0
    )
    same = ids_col == to_row(ids_col)

    own_line = jnp.sum(jnp.where(iota((dp, 128), 0) == me, tok, 0.0), axis=0, keepdims=True)
    at_lane = iota((tokens, 128), 0) + (me & (128 // tokens - 1)) * tokens
    target_col = jnp.sum(
        jnp.where(iota((tokens, 128), 1) == at_lane, own_line, 0.0), axis=1, keepdims=True
    )
    target = to_row(target_col)
    before = iota((tokens, tokens), 0) < iota((tokens, tokens), 1)
    order = jnp.sum(
        jnp.where(jnp.logical_and(target_col == target, before), 1.0, 0.0), axis=0, keepdims=True
    )
    token_slot = to_col(target * token_rows + order * 4)
    of_row = iota((tokens, rows_own), 1) >> 2
    slot_row = jnp.sum(
        jnp.where(iota((tokens, rows_own), 0) == of_row, token_slot, 0.0), axis=0, keepdims=True
    ).astype(jnp.int32) + (iota((1, rows_own), 1) & 3)
    taken = pick(iota((lm_rows, rows_own), 0) == slot_row)
    sent_id = owner_of((lm_rows, rows_own), 0, token_rows) * token_rows + (
        iota((lm_rows, rows_own), 0) & (token_rows - 1)
    )
    given = pick(sent_id == slot_row)

    for i in range(1, nt):
        gather(0, x_all, i).wait_recv()
    x = x_all[...].astype(f32)
    inv_first = lax.rsqrt(jnp.sum(x * x, axis=0, keepdims=True) / width + EPS)
    normed_in = (x * inv_first * gain_col[...]).astype(bf16)
    lhs[0] = normed_in

    def lend(kind, i):
        return copy(
            lhs.at[kind], lhs_in.at[y], y_ss.at[0, i - 1], y_rs.at[0, i - 1], dev(z, y + i)
        )

    def lend_to(kind):
        for i in range(1, ny):
            last = lax.rem(y + i, ny) == ny - 1

            @pl.when(last if kind else jnp.logical_not(last))
            def _(i=i):
                lend(kind, i).start()

    lend_to(0)
    packed = dot(wqkv_t[...], normed_in).astype(bf16)

    kept = []
    for h in range(heads):
        q, k, v = (packed[(3 * h + s) * HD : (3 * h + s + 1) * HD] for s in range(3))
        scores = jnp.where(same, dot(k, q, 0, 0) * scaling, -jnp.inf)
        raised = jnp.exp(scores - jnp.max(scores, axis=0, keepdims=True))
        weights = raised / jnp.sum(raised, axis=0, keepdims=True)
        rounded = weights.astype(bf16)
        at = pl.ds(pl.multiple_of(rank * features + h * HD, 16), HD)
        attn_all[at, :] = dot(v, rounded).astype(bf16)
        kept.append((q, k, v, weights, rounded))

    for i in range(1, nt):
        gather(1, attn_all, i).start()
    landed(1, cot_mid, cot_in)
    returned = cot_in[...].astype(f32).reshape(lm_rows, features).astype(bf16)
    upstream = dot(returned, taken, 0, 0)
    for i in range(1, nt):
        gather(1, attn_all, i).wait_recv()

    attn = attn_all[...]
    lhs[1] = attn
    lend_to(1)
    kind_here = jnp.where(y == ny - 1, 1, 0)
    lhs_in[y] = lhs[kind_here]
    residual = x_own + dot(wout_t[...], attn)
    lifted = merge_gain * upstream
    sums = [
        jnp.sum(residual * residual, axis=0, keepdims=True),
        jnp.sum(lifted * residual, axis=0, keepdims=True),
    ]
    stat_all[rank] = jnp.concatenate(sums + [jnp.zeros((6, rows_own), f32)], axis=0)

    def stat(i):
        at = stat_all.at[rank]
        return copy(at, at, t_ss.at[2, i - 1], t_rs.at[2, i - 1], mate(i))

    for i in range(1, nt):
        stat(i).start()
    for i in range(1, nt):
        stat(i).wait_recv()
    stats = jnp.sum(stat_all[...], axis=0)
    inv_second = lax.rsqrt(stats[0:1] / width + EPS)
    along = stats[1:2]
    scaled = residual * inv_second
    dresidual = (
        lifted * inv_second - residual * (along * (inv_second * inv_second * inv_second) / width)
    ).astype(bf16)
    spread[...] = dot(wout[...], dresidual).astype(bf16)

    def share(i):
        to = lax.rem(rank + i, nt)
        src = spread.at[pl.ds(pl.multiple_of(to * features, 16), features), :]
        return copy(src, grad_in.at[rank], t_ss.at[3, i - 1], t_rs.at[3, i - 1], mate(i))

    for i in range(1, nt):
        share(i).start()
    grad_in[rank] = spread[own, :]

    normed = (scaled * merge_gain).astype(bf16)
    tok_out[...] = dot(given, normed, 1, 1).reshape(tok_out.shape).astype(bf16)
    first_hop(2, tok_out, tok_mid)

    gains = jnp.sum(upstream * scaled, axis=1, keepdims=True)
    lane, sub = iota((features, 128), 1), iota((features, 128), 0)
    head = jnp.sum(jnp.where(lane == sub, gains, 0.0), axis=0, keepdims=True)
    tail = jnp.sum(jnp.where(lane + 128 == sub, gains, 0.0), axis=0, keepdims=True)
    gain_tile = jnp.concatenate([head, tail, jnp.zeros((14, 128), f32)], axis=0).astype(bf16)
    for s in range(ny):
        rhs[s, features : features + 16] = gain_tile
    rhs[ny - 1, 0:features] = dresidual

    second_hop(2, tok_out, tok_mid, tok_in)
    for i in range(1, nt):
        share(i).wait_recv()
    total = grad_in[0].astype(f32)
    for r in range(1, nt):
        total = total + grad_in[r].astype(f32)
    attn_grad = total.astype(bf16)

    for h in range(heads):
        q, k, v, weights, rounded = kept[h]
        g = attn_grad[h * HD : (h + 1) * HD]
        dprobs = dot(v, g, 0, 0)
        row_dot = jnp.sum(weights * dprobs, axis=0, keepdims=True)
        dscores = (weights * (dprobs - row_dot)).astype(bf16)
        grads = (
            (dot(k, dscores) * scaling).astype(bf16),
            (dot(q, dscores, 1, 1) * scaling).astype(bf16),
            dot(g, rounded, 1, 1).astype(bf16),
        )
        for s in range(3):
            line, half = (3 * h + s) // 2, (3 * h + s) % 2
            rhs[line, HD * half : HD * half + HD] = grads[s]

    def place_tokens():
        landed(2, tok_mid, tok_in)
        n = lm_rows
        owner = iota((n, dp), 0) >> log(token_rows)
        start = jnp.sum(jnp.where(iota((n, dp), 1) < owner, lm_row, 0.0), axis=1, keepdims=True)
        count = jnp.sum(jnp.where(iota((n, dp), 1) == owner, lm_row, 0.0), axis=1, keepdims=True)
        slot = (iota((n, 1), 0) & (token_rows - 1)) >> 2
        to = jnp.where(slot < count.astype(jnp.int32), start.astype(jnp.int32) + slot, -1)
        got = tok_in[...].astype(f32).reshape(n, features).astype(bf16)
        for quart in range(4):
            to_q = jnp.where((iota((n, 1), 0) & 3) == quart, to, -1)
            put = pick(iota((n, n // 4), 1) == to_q)
            merged_ref[quart] = dot(got, put, 0, 0).astype(bf16)

    def owed(i):
        to = lax.rem(y + i, ny)
        return copy(rhs.at[to], rhs_in.at[y], y_ss.at[1, i - 1], y_rs.at[1, i - 1], dev(z, y + i))

    for i in range(1, ny):
        owed(i).start()
    rhs_in[y] = rhs[y]
    live = (features // 16) * (width // 128)
    tiles = part.shape[0]
    per = tiles // nz
    block = per * groups
    part[pl.ds(live, tiles - live)] = jnp.zeros((tiles - live, 16, 128), bf16)
    for i in range(1, ny):
        lend(0, i).wait_recv()
    for i in range(1, ny):
        owed(i).wait_recv()
    left = jnp.concatenate([rhs_in[o, 0:features] for o in range(ny)], axis=1)
    for c in range(width // 128):
        right = jnp.concatenate([lhs_in[o, 128 * c : 128 * c + 128] for o in range(ny)], axis=1)
        lot = features // 16
        part[lot * c : lot * c + lot] = dot(left, right, 1, 1).astype(bf16).reshape(lot, 16, 128)
    gained = rhs_in[0, features : features + 16].astype(f32)
    for o in range(1, ny):
        gained = gained + rhs_in[o, features : features + 16].astype(f32)
    part[live] = gained.astype(bf16)

    steps = (2, 1, nz - 1)
    kin, place = lax.rem(z, 4), z // 4

    def class_of(step):
        return lax.rem(z + step, 4)

    def near(j):
        src = part.at[pl.ds(class_of(steps[j]) * block, block)]
        return copy(src, near_in.at[j], z_ss.at[0, j], z_rs.at[0, j], dev(z + steps[j], y))

    def apart(j):
        to = lax.rem(place + j, groups)
        src = class_sum.at[pl.ds(to * per, per)]
        return copy(
            src, apart_in.at[j - 1], z_ss.at[1, j - 1], z_rs.at[1, j - 1], dev(z + 4 * j, y)
        )

    for j in range(3):
        near(j).start()
    total = part[pl.ds(kin * block, block)].astype(f32)
    for j in range(3):
        near(j).wait_recv()
        total = total + near_in[j].astype(f32)
    class_sum[...] = total.astype(bf16)
    for j in range(1, groups):
        apart(j).start()
    total = class_sum[pl.ds(place * per, per)].astype(f32)
    for j in range(1, groups):
        apart(j).wait_recv()
        total = total + apart_in[j - 1].astype(f32)
    own_part = pl.ds(kin * block + place * per, per)
    full[y, own_part] = total.astype(bf16)

    def give_apart(j):
        at = full.at[y, own_part]
        return copy(at, at, g_ss.at[0, j - 1], g_rs.at[0, j - 1], dev(z + 4 * j, y))

    def give_near(j):
        at = full.at[y, pl.ds(kin * block, block)]
        return copy(at, at, g_ss.at[1, j], g_rs.at[1, j], dev(z + steps[j], y))

    def give_y(j, i):
        kind = kin if j == 3 else lax.rem(z + nz - steps[j], 4)
        at = full.at[y, pl.ds(kind * block, block)]
        return copy(at, at, g_ss.at[2 + j, i - 1], g_rs.at[2 + j, i - 1], dev(z, y + i))

    for j in range(1, groups):
        give_apart(j).start()
    place_tokens()
    for j in range(1, groups):
        give_apart(j).wait_recv()
    for j in (1, 2, 0):
        give_near(j).start()
    for i in range(1, ny):
        give_y(3, i).start()
    for j in (1, 2, 0):
        give_near(j).wait_recv()
        for i in range(1, ny):
            give_y(j, i).start()
    for j in (3, 1, 2, 0):
        for i in range(1, ny):
            give_y(j, i).wait_recv()

    lot = features // 16
    for s in range(ny):
        for c in range(width // 128):
            got = full[s, lot * c : lot * c + lot].reshape(features, 128)
            lanes = slice(128 * c, 128 * c + 128)
            if s < ny - 1:
                qkv_ref[features * s : features * s + features, lanes] = got
            else:
                out_ref[:, lanes] = got
    line = full[0, live].astype(f32)
    gsum_ref[:, 0:128] = line[0:1]
    gsum_ref[:, 128:features] = line[1:2, 0 : features - 128]

    for k, (out, mid, got) in enumerate(
        ((row_out, row_mid, row_in), (cot_out, cot_mid, cot_in), (tok_out, tok_mid, tok_in))
    ):
        for i in range(1, ny):
            hop(k, out, mid, i).wait_send()

        def drain(i, carry, k=k, mid=mid, got=got):
            far(k, mid, got, i).wait_send()
            return carry

        lax.fori_loop(1, nz, drain, 0)
    for i in range(1, nt):
        gather(0, x_all, i).wait_send()
        gather(1, attn_all, i).wait_send()
        stat(i).wait_send()
        share(i).wait_send()
    for i in range(1, ny):
        lend(0, i).wait_send()
        owed(i).wait_send()
        for j in range(4):
            give_y(j, i).wait_send()
    for j in range(3):
        near(j).wait_send()
        give_near(j).wait_send()
    for j in range(1, groups):
        apart(j).wait_send()
        give_apart(j).wait_send()


def body(
    patches,
    send_counts,
    window_ids,
    token_shard,
    first_gain,
    qkv_weight,
    out_weight,
    merge_gain,
    cotangent,
):
    bf16, f32 = jnp.bfloat16, jnp.float32
    dp, nt = lax.axis_size("dp"), lax.axis_size("tensor")
    ny = NY
    nz = dp // ny
    rows_src, features = patches.shape
    rows_own = rows_src // 2
    lm_slots = cotangent.shape[0]
    lm_rows = 4 * lm_slots
    width = first_gain.shape[0]
    packed = qkv_weight.shape[1]
    live = (features // 16) * (width // 128)
    per = -(-(live + 1) // nz)
    groups = nz // 4
    vmem = pl.BlockSpec(memory_space=pltpu.VMEM)
    sems = pltpu.SemaphoreType.DMA

    def held(*shape, dtype=bf16):
        return pltpu.VMEM(shape, dtype)

    def legs(rows):
        out = held(ny, nz, rows, features)
        return [out, out, held(nz, ny, rows, features)]

    merged, qkv_grad, out_grad, gain_sum = pl.pallas_call(
        functools.partial(layer_kernel, nz, ny),
        out_shape=(
            jax.ShapeDtypeStruct((4, features, lm_slots), bf16),
            jax.ShapeDtypeStruct((packed, width), bf16),
            jax.ShapeDtypeStruct((features, width), bf16),
            jax.ShapeDtypeStruct((1, features), f32),
        ),
        in_specs=[vmem] * 9,
        out_specs=(vmem,) * 4,
        scratch_shapes=[
            *legs(rows_src // dp),
            *legs(lm_rows // dp),
            *legs(lm_rows // dp),
            held(width, rows_own),
            held(width, rows_own),
            held(nt, 8, rows_own, dtype=f32),
            held(width, rows_own),
            held(nt, features, rows_own),
            held(width, features),
            held(width, 1, dtype=f32),
            held(2, width, rows_own),
            held(ny, width, rows_own),
            held(ny, features + 16, rows_own),
            held(ny, features + 16, rows_own),
            held(per * nz, 16, 128),
            held(3, per * groups, 16, 128),
            held(per * groups, 16, 128),
            held(max(groups - 1, 1), per, 16, 128),
            held(ny, per * nz, 16, 128),
            sems((3, ny - 1)),
            sems((3, ny - 1)),
            sems((3, nz - 1)),
            sems((3, nz - 1)),
            sems((4, nt - 1)),
            sems((4, nt - 1)),
            sems((2, ny - 1)),
            sems((2, ny - 1)),
            sems((2, 3)),
            sems((2, 3)),
            sems((6, 3)),
            sems((6, 3)),
        ],
        compiler_params=pltpu.CompilerParams(
            collective_id=0, has_side_effects=True, vmem_limit_bytes=56 * 1024 * 1024
        ),
        name="layer",
    )(
        patches.T,
        send_counts,
        window_ids,
        token_shard.reshape(1, token_shard.shape[0]),
        first_gain,
        qkv_weight.T,
        out_weight.T,
        merge_gain.reshape(1, features),
        cotangent.transpose(1, 2, 0),
    )
    return (
        merged.transpose(2, 0, 1),
        qkv_grad.T,
        out_grad.T,
        gain_sum.reshape(features),
    )


def solution(mesh):
    placed = (
        P("dp", "tensor"),
        P(),
        P("dp", None),
        P(),
        P(),
        P(None, "tensor"),
        P(None, "tensor"),
        P("tensor"),
        P("dp", None, "tensor"),
    )
    return jax.shard_map(
        body,
        mesh=mesh,
        in_specs=placed,
        out_specs=(P("dp", None, "tensor"), P(None, "tensor"), P(None, "tensor"), P("tensor")),
        check_vma=False,
    )
```

time: 151 us -> 132 us (0.87)
  local copies, waits for them, and re-layouts: 16 us -> 5.36 us
  Pallas kernels: 130 us -> 125 us
  other arithmetic: 2.24 us -> 0 us
    pallas_call x1, Pallas kernels: 130 us -> 125 us  [body(): pl.pallas_call(functools.partial(layer_kernel, nz, ny), out_shape=(jax.Sh...]
    unnamed x14 -> x8, local copies, waits for them, and re-layouts: 10.2 us -> 5.36 us
    reshape x5 -> x0, local copies, waits for them, and re-layouts: 4.56 us -> none  [the longest x1 1.29 us: body(): first_gain.reshape(1, width)]
where the time goes in v3:
time: 132 us; the launch traced here: 131 us
  Pallas kernels  125 us (95%)
  local copies, waits for them, and re-layouts  5.36 us (4%)
    pallas_call x1, Pallas kernels, body(): pl.pallas_call(functools.partial(layer_kernel, nz, ny), out_shape=(jax.Sh...  125 us
    unnamed x8, local copies, waits for them, and re-layouts  5.36 us

profile of v3, /device:TPU:6, one launch (start us, length us, event | category | flops | bytes accessed | tf_op | source)
XLA Modules:
  0.0 130.8 jit_solution(12737252985785578933)
XLA Ops:
  0.6 124.8 %layer.1 = (bf16[4,160,128]{2,1,0:T(8,128)(2,1)}, bf16[480,1280]{1,0:T(8,128)(2,1)}, bf16[160,1280]{1,0:T(8,128)(2,1)}, f32[1,160]{1,0:T(1,128)}) custom-call(bf16[160,256]{1,0:T(8,128)(2,1)} %bitcast.16, s32[64,64]{1,0:T(8,128)} %counts_ref.1, s32[2,64]{1,0:T(2,128)} %ids_ref.1, s32[1,2048]{1,0:T(1,128)} %bitcast.17, f32[1280]{0:T(1024)} %gain1_ref.1, ...), custom_call_target="tpu_custom_call" | custom-call | tf_op jit(solution)/shard_map/layer/pallas_call | solution.py:565
  125.4 1.6 %copy.17 = bf16[128,4,160]{0,2,1:T(8,128)(2,1)} copy(bf16[128,4,160]{0,2,1:T(8,128)(2,1)} %bitcast.15) | data formatting | bytes 327680
  127.0 0.0 copy-start
  127.0 0.0 copy-start.1
  127.0 2.4 %copy.18 = bf16[1280,480]{0,1:T(8,128)(2,1)} copy(bf16[1280,480]{0,1:T(8,128)(2,1)} %bitcast.11) | data formatting | bytes 2457600
  129.4 0.0 copy-done
  129.5 0.8 copy.19
  130.2 0.0 copy-done.1
  130.2 0.6 copy.20
Async XLA Ops:
  127.0 2.5 %copy-start = (bf16[160,1280]{1,0:T(8,128)(2,1)S(1)}, bf16[160,1280]{1,0:T(8,128)(2,1)}, u32[]{:S(2)}) copy-start(bf16[160,1280]{1,0:T(8,128)(2,1)} %get-tuple-element.10) | copy-start | bytes 1228804
  127.0 3.2 %copy-start.1 = (f32[1,160]{1,0:T(1,128)S(1)}, f32[1,160]{1,0:T(1,128)}, u32[]{:S(2)}) copy-start(f32[1,160]{1,0:T(1,128)} %get-tuple-element.11) | copy-start | bytes 1924

commit v4 on v3

--- a/solution.py
+++ b/solution.py
@@ -56,9 +56,7 @@
     gain2_ref,
     cot_ref,
     merged_ref,
-    qkv_ref,
-    out_ref,
-    gsum_ref,
+    tiles_ref,
     row_out,
     row_mid,
     row_in,
@@ -123,12 +121,14 @@
         return {"tensor": lax.rem(rank + i, nt)}
 
     barrier = pltpu.get_barrier_semaphore()
+    distant = sorted(range(1, nz), key=lambda i: -min(i, nz - i))
+    plain = list(range(1, nz))
+    for i in distant:
+        pl.semaphore_signal(barrier, inc=1, device_id=dev(z + i, y), device_id_type=MESH)
     for i in range(1, ny):
         pl.semaphore_signal(barrier, inc=1, device_id=dev(z, y + i), device_id_type=MESH)
     for i in range(1, nt):
         pl.semaphore_signal(barrier, inc=1, device_id=mate(i), device_id_type=MESH)
-    for i in range(1, nz):
-        pl.semaphore_signal(barrier, inc=1, device_id=dev(z + i, y), device_id_type=MESH)
 
     def owner_of(shape, dim, per):
         at = iota(shape, dim) >> log(per)
@@ -149,15 +149,14 @@
             hop(k, out, mid, i).start()
         mid[y] = out[y]
 
-    def second_hop(k, out, mid, got):
+    def onward(k, mid, got, order):
+        for i in order:
+            far(k, mid, got, i).start()
+
+    def second_hop(k, out, mid, got, order):
         for i in range(1, ny):
             hop(k, out, mid, i).wait_recv()
-
-        def send(i, carry):
-            far(k, mid, got, i).start()
-            return carry
-
-        lax.fori_loop(1, nz, send, 0)
+        onward(k, mid, got, order)
         got[z] = mid[:, z]
 
     def landed(k, mid, got):
@@ -177,9 +176,6 @@
     slot = iota((n, 1), 0) & (slot_cap - 1)
     chosen = pick(iota((n, rows_src), 1) == jnp.minimum(start + slot, rows_src - 1))
     row_out[...] = dot(chosen, patches_ref[...], 1, 1).reshape(row_out.shape).astype(bf16)
-
-    pl.semaphore_wait(barrier, ny - 1 + nt - 1 + nz - 1)
-    first_hop(0, row_out, row_mid)
 
     lines = tok_ref.shape[1] // 128
     tok = jnp.concatenate([tok_ref[:, 128 * a : 128 * a + 128] for a in range(lines)], axis=0)
@@ -205,7 +201,9 @@
         total = total + dot(pick(iota((n, lm_rows // 4), 1) == place_q), cot_ref[quart], 1, 1)
     cot_out[...] = total.reshape(cot_out.shape).astype(bf16)
 
-    second_hop(0, row_out, row_mid, row_in)
+    pl.semaphore_wait(barrier, ny - 1 + nt - 1 + nz - 1)
+    first_hop(0, row_out, row_mid)
+    second_hop(0, row_out, row_mid, row_in, plain)
     first_hop(1, cot_out, cot_mid)
 
     n = rows_src
@@ -220,7 +218,7 @@
     where_to = jnp.where(slot < count.astype(jnp.int32), start.astype(jnp.int32) + slot, -1)
     placed = pick(iota((n, rows_own), 1) == where_to)
 
-    second_hop(1, cot_out, cot_mid, cot_in)
+    second_hop(1, cot_out, cot_mid, cot_in, plain)
 
     landed(0, row_mid, row_in)
     own = pl.ds(pl.multiple_of(rank * features, 16), features)
@@ -360,7 +358,8 @@
         rhs[s, features : features + 16] = gain_tile
     rhs[ny - 1, 0:features] = dresidual
 
-    second_hop(2, tok_out, tok_mid, tok_in)
+    split = 5
+    second_hop(2, tok_out, tok_mid, tok_in, distant[:split])
     for i in range(1, nt):
         share(i).wait_recv()
     total = grad_in[0].astype(f32)
@@ -429,75 +428,93 @@
     def class_of(step):
         return lax.rem(z + step, 4)
 
-    def near(j):
-        src = part.at[pl.ds(class_of(steps[j]) * block, block)]
-        return copy(src, near_in.at[j], z_ss.at[0, j], z_rs.at[0, j], dev(z + steps[j], y))
-
-    def apart(j):
-        to = lax.rem(place + j, groups)
-        src = class_sum.at[pl.ds(to * per, per)]
+    def chunk(kind, group):
+        return pl.ds(kind * block + group * per, per)
+
+    def turn(zz, o):
+        return lax.rem(lax.rem(zz + nz, nz) // 4 + o, groups)
+
+    def near(j, group):
         return copy(
-            src, apart_in.at[j - 1], z_ss.at[1, j - 1], z_rs.at[1, j - 1], dev(z + 4 * j, y)
+            part.at[chunk(class_of(steps[j]), group)],
+            near_in.at[group, j],
+            z_ss.at[j, group],
+            z_rs.at[j, group],
+            dev(z + steps[j], y),
         )
 
-    for j in range(3):
-        near(j).start()
-    total = part[pl.ds(kin * block, block)].astype(f32)
-    for j in range(3):
-        near(j).wait_recv()
-        total = total + near_in[j].astype(f32)
-    class_sum[...] = total.astype(bf16)
-    for j in range(1, groups):
-        apart(j).start()
-    total = class_sum[pl.ds(place * per, per)].astype(f32)
-    for j in range(1, groups):
-        apart(j).wait_recv()
-        total = total + apart_in[j - 1].astype(f32)
-    own_part = pl.ds(kin * block + place * per, per)
-    full[y, own_part] = total.astype(bf16)
-
-    def give_apart(j):
-        at = full.at[y, own_part]
-        return copy(at, at, g_ss.at[0, j - 1], g_rs.at[0, j - 1], dev(z + 4 * j, y))
-
-    def give_near(j):
-        at = full.at[y, pl.ds(kin * block, block)]
-        return copy(at, at, g_ss.at[1, j], g_rs.at[1, j], dev(z + steps[j], y))
-
-    def give_y(j, i):
-        kind = kin if j == 3 else lax.rem(z + nz - steps[j], 4)
-        at = full.at[y, pl.ds(kind * block, block)]
-        return copy(at, at, g_ss.at[2 + j, i - 1], g_rs.at[2 + j, i - 1], dev(z, y + i))
-
-    for j in range(1, groups):
-        give_apart(j).start()
+    def apart(o):
+        src = class_sum.at[turn(z, o)]
+        return copy(
+            src, apart_in.at[o - 1], z_ss.at[3, o - 1], z_rs.at[3, o - 1], dev(z + 4 * o, y)
+        )
+
+    outward = sorted(range(groups), key=lambda o: min(o, groups - o))
+    inward = outward[::-1]
+    for o in inward:
+        for j in range(3):
+            near(j, turn(z + steps[j], o)).start()
+    for o in inward:
+        group = turn(z, o)
+        total = part[chunk(kin, group)].astype(f32)
+        for j in range(3):
+            near(j, group).wait_recv()
+            total = total + near_in[group, j].astype(f32)
+        if o:
+            class_sum[group] = total.astype(bf16)
+            apart(o).start()
+    onward(2, tok_mid, tok_in, distant[split:])
+    for o in inward[:-1]:
+        apart(o).wait_recv()
+        total = total + apart_in[o - 1].astype(f32)
+    full[y, chunk(kin, place)] = total.astype(bf16)
+
+    def give_apart(o):
+        at = full.at[y, chunk(kin, place)]
+        return copy(at, at, g_ss.at[0, o - 1], g_rs.at[0, o - 1], dev(z + 4 * o, y))
+
+    def give_near(o, j):
+        at = full.at[y, chunk(kin, turn(z, groups - o))]
+        return copy(at, at, g_ss.at[1 + o, j], g_rs.at[1 + o, j], dev(z + steps[j], y))
+
+    def give_y(o, j, i):
+        zz = z if j == 3 else z - steps[j]
+        at = full.at[y, chunk(lax.rem(zz + nz, 4), turn(zz, groups - o))]
+        k = 1 + groups + 4 * o + j
+        return copy(at, at, g_ss.at[k, i - 1], g_rs.at[k, i - 1], dev(z, y + i))
+
+    def send_on(o):
+        for j in (1, 2, 0):
+            give_near(o, j).start()
+        for i in range(1, ny):
+            give_y(o, 3, i).start()
+
+    def from_near(o):
+        for j in (1, 2, 0):
+            give_near(o, j).wait_recv()
+            for i in range(1, ny):
+                give_y(o, j, i).start()
+
+    for o in inward[:-1]:
+        give_apart(o).start()
+    send_on(0)
+    from_near(0)
+    for o in outward[1:-1]:
+        give_apart(o).wait_recv()
+        send_on(o)
+    for o in outward[1:-1]:
+        from_near(o)
+    for o in outward[1:][-1:]:
+        give_apart(o).wait_recv()
+        send_on(o)
+        from_near(o)
     place_tokens()
-    for j in range(1, groups):
-        give_apart(j).wait_recv()
-    for j in (1, 2, 0):
-        give_near(j).start()
-    for i in range(1, ny):
-        give_y(3, i).start()
-    for j in (1, 2, 0):
-        give_near(j).wait_recv()
-        for i in range(1, ny):
-            give_y(j, i).start()
-    for j in (3, 1, 2, 0):
-        for i in range(1, ny):
-            give_y(j, i).wait_recv()
-
-    lot = features // 16
-    for s in range(ny):
-        for c in range(width // 128):
-            got = full[s, lot * c : lot * c + lot].reshape(features, 128)
-            lanes = slice(128 * c, 128 * c + 128)
-            if s < ny - 1:
-                qkv_ref[features * s : features * s + features, lanes] = got
-            else:
-                out_ref[:, lanes] = got
-    line = full[0, live].astype(f32)
-    gsum_ref[:, 0:128] = line[0:1]
-    gsum_ref[:, 128:features] = line[1:2, 0 : features - 128]
+    for o in outward:
+        for j in (3, 1, 2, 0):
+            for i in range(1, ny):
+                give_y(o, j, i).wait_recv()
+
+    tiles_ref[...] = full[...]
 
     for k, (out, mid, got) in enumerate(
         ((row_out, row_mid, row_in), (cot_out, cot_mid, cot_in), (tok_out, tok_mid, tok_in))
@@ -518,14 +535,35 @@
     for i in range(1, ny):
         lend(0, i).wait_send()
         owed(i).wait_send()
-        for j in range(4):
-            give_y(j, i).wait_send()
-    for j in range(3):
-        near(j).wait_send()
-        give_near(j).wait_send()
-    for j in range(1, groups):
-        apart(j).wait_send()
-        give_apart(j).wait_send()
+        for o in range(groups):
+            for j in range(4):
+                give_y(o, j, i).wait_send()
+    for o in range(groups):
+        for j in range(3):
+            near(j, turn(z + steps[j], o)).wait_send()
+            give_near(o, j).wait_send()
+    for o in range(1, groups):
+        apart(o).wait_send()
+        give_apart(o).wait_send()
+
+
+def spread_kernel(tiles_ref, merged_ref, placed_ref, qkv_ref, out_ref, gsum_ref):
+    ny, tiles = tiles_ref.shape[0], tiles_ref.shape[1]
+    features, width = out_ref.shape
+    lot = features // 16
+    live = lot * (width // 128)
+    for s in range(ny):
+        for c in range(width // 128):
+            got = tiles_ref[s, lot * c : lot * c + lot].reshape(features, 128)
+            lanes = slice(128 * c, 128 * c + 128)
+            if s < ny - 1:
+                qkv_ref[features * s : features * s + features, lanes] = got
+            else:
+                out_ref[:, lanes] = got
+    line = tiles_ref[0, live].astype(jnp.float32)
+    gsum_ref[:, 0:128] = line[0:1]
+    gsum_ref[:, 128:features] = line[1:2, 0 : features - 128]
+    placed_ref[...] = merged_ref[...]
 
 
 def body(
@@ -562,16 +600,14 @@
         out = held(ny, nz, rows, features)
         return [out, out, held(nz, ny, rows, features)]
 
-    merged, qkv_grad, out_grad, gain_sum = pl.pallas_call(
+    merged, tiles = pl.pallas_call(
         functools.partial(layer_kernel, nz, ny),
         out_shape=(
             jax.ShapeDtypeStruct((4, features, lm_slots), bf16),
-            jax.ShapeDtypeStruct((packed, width), bf16),
-            jax.ShapeDtypeStruct((features, width), bf16),
-            jax.ShapeDtypeStruct((1, features), f32),
+            jax.ShapeDtypeStruct((ny, per * nz, 16, 128), bf16),
         ),
         in_specs=[vmem] * 9,
-        out_specs=(vmem,) * 4,
+        out_specs=(vmem,) * 2,
         scratch_shapes=[
             *legs(rows_src // dp),
             *legs(lm_rows // dp),
@@ -588,8 +624,8 @@
             held(ny, features + 16, rows_own),
             held(ny, features + 16, rows_own),
             held(per * nz, 16, 128),
-            held(3, per * groups, 16, 128),
-            held(per * groups, 16, 128),
+            held(groups, 3, per, 16, 128),
+            held(groups, per, 16, 128),
             held(max(groups - 1, 1), per, 16, 128),
             held(ny, per * nz, 16, 128),
             sems((3, ny - 1)),
@@ -600,10 +636,10 @@
             sems((4, nt - 1)),
             sems((2, ny - 1)),
             sems((2, ny - 1)),
-            sems((2, 3)),
-            sems((2, 3)),
-            sems((6, 3)),
-            sems((6, 3)),
+            sems((4, max(groups, 3))),
+            sems((4, max(groups, 3))),
+            sems((1 + 5 * groups, 3)),
+            sems((1 + 5 * groups, 3)),
         ],
         compiler_params=pltpu.CompilerParams(
             collective_id=0, has_side_effects=True, vmem_limit_bytes=56 * 1024 * 1024
@@ -620,6 +656,18 @@
         merge_gain.reshape(1, features),
         cotangent.transpose(1, 2, 0),
     )
+    merged, qkv_grad, out_grad, gain_sum = pl.pallas_call(
+        spread_kernel,
+        out_shape=(
+            jax.ShapeDtypeStruct((4, features, lm_slots), bf16),
+            jax.ShapeDtypeStruct((packed, width), bf16),
+            jax.ShapeDtypeStruct((features, width), bf16),
+            jax.ShapeDtypeStruct((1, features), f32),
+        ),
+        in_specs=[vmem] * 2,
+        out_specs=(vmem,) * 4,
+        name="spread",
+    )(tiles, merged)
     return (
         merged.transpose(2, 0, 1),
         qkv_grad.T,

time: 132 us -> 124 us (0.939)
  the two profiles are of different devices: /device:TPU:6 before, /device:TPU:32 now
where the time goes in v4:
time: 124 us
  Pallas kernels  123 us (99%)
    pallas_call x1, Pallas kernels, body(): pl.pallas_call(functools.partial(layer_kernel, nz, ny), out_shape=(jax.Sh...  120 us
    pallas_call x1, Pallas kernels, body(): pl.pallas_call(spread_kernel, out_shape=(jax.ShapeDtypeStruct((4, feature...  3 us

profile of v4, /device:TPU:32, one launch (start us, length us, event | category | flops | bytes accessed | tf_op | source)
XLA Modules:
  0.0 123.8 jit_solution(11747206931110118844)
XLA Ops:
  0.6 120.2 %layer.1 = (bf16[4,160,128]{2,1,0:T(8,128)(2,1)}, bf16[4,112,16,128]{3,2,1,0:T(8,128)(2,1)}) custom-call(bf16[160,256]{1,0:T(8,128)(2,1)} %bitcast.13, s32[64,64]{1,0:T(8,128)} %counts_ref.1, s32[2,64]{1,0:T(2,128)} %ids_ref.1, s32[1,2048]{1,0:T(1,128)} %bitcast.14, f32[1280]{0:T(1024)} %gain1_ref.1, bf16[480,1280]{1,0:T(8,128)(2,1)} %bitcast.10, ...), custom_call_target="tpu_custom_call" | custom-call | tf_op jit(solution)/shard_map/layer/pallas_call | solution.py:603
  120.8 3.0 %spread.1 = (bf16[4,160,128]{2,1,0:T(8,128)(2,1)}, bf16[480,1280]{1,0:T(8,128)(2,1)}, bf16[160,1280]{1,0:T(8,128)(2,1)}, f32[1,160]{1,0:T(1,128)}) custom-call(bf16[4,112,16,128]{3,2,1,0:T(8,128)(2,1)} %get-tuple-element.10.tiles_ref, bf16[4,160,128]{2,1,0:T(8,128)(2,1)} %get-tuple-element.11.merged_ref), custom_call_target="tpu_custom_call" | custom-call | tf_op jit(solution)/shard_map/spread/pallas_call | solution.py:659
